TPU v7x, 32 devices: a whole 2x2x4 slice. The times are simulated.
32 devices in a mesh: dp: 8 (over y, x, core), seq: 4 (over z).
Axes of the slice: x: 2, y: 2, z: 4, core: 2. Of those that a mesh axis runs over, the one named last changes fastest.
Arguments:
- inputs: bfloat16 [8, 1040, 1024], P('dp', 'seq')
- cotangent: bfloat16 [8, 1040, 1024], P('dp', 'seq'), may hold values from -6 to 6
- valid_len: int32 [8], P('dp'), may hold values from 520 to 1025, as said below
- ln1_gain: bfloat16 [1024], P('dp'), may hold values from 0.099609375 to 1.8984375
- ln1_bias: bfloat16 [1024], P('dp'), may hold values from -3 to 3
- w_qkv: bfloat16 [1024, 3072], P('dp')
- b_qv: bfloat16 [2048], P('dp'), may hold values from -3 to 3
- w_out: bfloat16 [1024, 1024], P('dp'), may hold values from -2 to 2
- b_out: bfloat16 [1024], P('dp'), may hold values from -3 to 3
- ln2_gain: bfloat16 [1024], P('dp'), may hold values from 0.099609375 to 1.8984375
- ln2_bias: bfloat16 [1024], P('dp'), may hold values from -3 to 3
- w_up: bfloat16 [1024, 4096], P('dp'), may hold values from -0.1875 to 0.1875
- b_up: bfloat16 [4096], P('dp'), may hold values from -3 to 3
- w_down: bfloat16 [4096, 1024], P('dp'), may hold values from -0.09375 to 0.09375
- b_down: bfloat16 [1024], P('dp'), may hold values from -3 to 3
Outputs:
- outputs: bfloat16 [8, 1040, 1024], P('dp', 'seq')
- d_inputs: bfloat16 [8, 1040, 1024], P('dp', 'seq')
- g_ln1_gain: float32 [1024], P('dp')
- g_ln1_bias: float32 [1024], P('dp')
- g_w_qkv: float32 [1024, 3072], P('dp')
- g_b_qv: float32 [2048], P('dp')
- g_w_out: float32 [1024, 1024], P('dp')
- g_b_out: float32 [1024], P('dp')
- g_ln2_gain: float32 [1024], P('dp')
- g_ln2_bias: float32 [1024], P('dp')
- g_w_up: float32 [1024, 4096], P('dp')
- g_b_up: float32 [4096], P('dp')
- g_w_down: float32 [4096, 1024], P('dp')
- g_b_down: float32 [1024], P('dp')
Inputs may be any that keep to these rules, and one draw needn't show every extreme that they name: `valid_len`: number of leading real tokens of each image; key slots at or after it are padding. Some image has exactly 1025 in every draw.
All inputs are finite; a program needn't handle non-finite values.
Results may differ from a plain program's by a relative error of at most 0.012.
The roundings to bfloat16 on the way count: a program that leaves them out, or rounds other values in their place, can miss the bound.
Values may be sent and summed in bfloat16 or wider, within the bound.
A program may use at most 192 MiB of HBM per device.

v0:
```python
import math

import jax
import jax.numpy as jnp
from jax import lax
from jax.sharding import PartitionSpec as P

HD = 64


EPSILON = 1e-05
ROOT_HALF = 0.7071067811865476
GAUSS_DENSITY = 0.3989422804014327
NEG_LARGE = -1e30


def norm_forward(values, gain_vec, shift_vec):
    mean_val = jnp.mean(values, axis=-1, keepdims=True)
    centred = values - mean_val
    inv_std = lax.rsqrt(jnp.mean(centred * centred, axis=-1, keepdims=True) + EPSILON)
    normed = centred * inv_std
    return (normed, inv_std, normed * gain_vec.astype(jnp.float32) + shift_vec.astype(jnp.float32))


def norm_backward(upstream, normed, inv_std, gain_vec):
    scaled = upstream * gain_vec.astype(jnp.float32)
    first_mean = jnp.mean(scaled, axis=-1, keepdims=True)
    second_mean = jnp.mean(scaled * normed, axis=-1, keepdims=True)
    return inv_std * (scaled - first_mean - normed * second_mean)


def gelu_value(preact):
    return 0.5 * preact * (1.0 + lax.erf(preact * ROOT_HALF))


def gelu_slope(preact):
    return (
        0.5 * (1.0 + lax.erf(preact * ROOT_HALF))
        + preact * jnp.exp(-0.5 * preact * preact) * GAUSS_DENSITY
    )


def against(left_mat, right_mat):
    return lax.dot_general(
        left_mat, right_mat, (((1,), (1,)), ((), ())), preferred_element_type=jnp.float32
    )


def outer_sum(left_mat, right_mat):
    return lax.dot_general(
        left_mat, right_mat, (((0,), (0,)), ((), ())), preferred_element_type=jnp.float32
    )


def scores_of(queries, keys, valid_count, factor):
    logits = jnp.einsum("qhe,khe->hqk", queries, keys, preferred_element_type=jnp.float32) * factor
    key_live = lax.iota(jnp.int32, keys.shape[0]) < valid_count
    return jnp.where(key_live[None, None, :], logits, NEG_LARGE)


def attend_forward(queries, keys, values_in, valid_count, factor):
    logits = scores_of(queries, keys, valid_count, factor)
    row_max = jnp.max(logits, axis=-1, keepdims=True)
    log_total = row_max + jnp.log(jnp.sum(jnp.exp(logits - row_max), axis=-1, keepdims=True))
    weights = jnp.exp(logits - log_total).astype(jnp.bfloat16)
    output = jnp.einsum("hqk,khe->qhe", weights, values_in, preferred_element_type=jnp.float32)
    return (output.astype(jnp.bfloat16), log_total)


def attend_backward(queries, keys, values_in, output, log_total, d_output, valid_count, factor):
    logits = scores_of(queries, keys, valid_count, factor)
    attn_probs = jnp.exp(logits - log_total)
    probs_bf = attn_probs.astype(jnp.bfloat16)
    d_values = jnp.einsum(
        "hqk,qhe->khe", probs_bf, d_output, preferred_element_type=jnp.float32
    ).astype(jnp.bfloat16)
    d_probs = jnp.einsum("qhe,khe->hqk", d_output, values_in, preferred_element_type=jnp.float32)
    row_dot = jnp.sum(d_output.astype(jnp.float32) * output.astype(jnp.float32), axis=-1)
    d_logits = (factor * attn_probs * (d_probs - jnp.transpose(row_dot)[:, :, None])).astype(
        jnp.bfloat16
    )
    d_queries = jnp.einsum(
        "hqk,khe->qhe", d_logits, keys, preferred_element_type=jnp.float32
    ).astype(jnp.bfloat16)
    d_keys = jnp.einsum(
        "hqk,qhe->khe", d_logits, queries, preferred_element_type=jnp.float32
    ).astype(jnp.bfloat16)
    return (d_queries, d_keys, d_values)


def shards(
    inputs,
    cotangent,
    valid_len,
    ln1_gain,
    ln1_bias,
    w_qkv,
    b_qv,
    w_out,
    b_out,
    ln2_gain,
    ln2_bias,
    w_up,
    b_up,
    w_down,
    b_down,
):
    images, shard_len, model_width = inputs.shape
    groups = lax.axis_size("seq")
    local_width = model_width // groups
    heads_local = local_width // HD
    factor = 1.0 / math.sqrt(HD)
    gathered = (
        lax.all_gather(ln1_gain, "dp", axis=0, tiled=True),
        lax.all_gather(ln1_bias, "dp", axis=0, tiled=True),
        lax.all_gather(w_qkv, "dp", axis=0, tiled=True),
        lax.all_gather(b_qv, "dp", axis=0, tiled=True),
        lax.all_gather(w_out, "dp", axis=0, tiled=True),
        lax.all_gather(b_out, "dp", axis=0, tiled=True),
        lax.all_gather(ln2_gain, "dp", axis=0, tiled=True),
        lax.all_gather(ln2_bias, "dp", axis=0, tiled=True),
        lax.all_gather(w_up, "dp", axis=0, tiled=True),
        lax.all_gather(b_up, "dp", axis=0, tiled=True),
        lax.all_gather(w_down, "dp", axis=0, tiled=True),
        lax.all_gather(b_down, "dp", axis=0, tiled=True),
    )
    (
        gain_one,
        bias_one,
        qkv_full,
        qv_bias,
        out_full,
        out_bias,
        gain_two,
        bias_two,
        up_full,
        up_bias,
        down_full,
        down_bias,
    ) = gathered
    token_rows = inputs.reshape(images * shard_len, model_width).astype(jnp.float32)
    normed_one, inv_one, pre_one = norm_forward(token_rows, gain_one, bias_one)
    hidden_one = pre_one.astype(jnp.bfloat16)
    qkv_bias = jnp.concatenate(
        [qv_bias[:model_width], jnp.zeros((model_width,), jnp.bfloat16), qv_bias[model_width:]]
    ).astype(jnp.float32)
    projected = (
        jnp.dot(hidden_one, qkv_full, preferred_element_type=jnp.float32) + qkv_bias
    ).astype(jnp.bfloat16)
    by_heads = lax.all_to_all(
        projected.reshape(images, shard_len, 3, model_width),
        "seq",
        split_axis=3,
        concat_axis=1,
        tiled=True,
    )
    seq_len = by_heads.shape[1]
    split_heads = by_heads.reshape(images, seq_len, 3, heads_local, HD)

    def forward_one(element):
        packed, live_count = element
        return attend_forward(packed[:, 0], packed[:, 1], packed[:, 2], live_count, factor)

    attended, log_totals = lax.map(forward_one, (split_heads, valid_len))
    merged = lax.all_to_all(
        attended.reshape(images, seq_len, local_width),
        "seq",
        split_axis=1,
        concat_axis=2,
        tiled=True,
    )
    merged_rows = merged.reshape(images * shard_len, model_width)
    residual = (
        token_rows
        + jnp.dot(merged_rows, out_full, preferred_element_type=jnp.float32)
        + out_bias.astype(jnp.float32)
    )
    normed_two, inv_two, pre_two = norm_forward(residual, gain_two, bias_two)
    hidden_two = pre_two.astype(jnp.bfloat16)
    preact = jnp.dot(hidden_two, up_full, preferred_element_type=jnp.float32) + up_bias.astype(
        jnp.float32
    )
    activated = gelu_value(preact).astype(jnp.bfloat16)
    result = (
        residual
        + jnp.dot(activated, down_full, preferred_element_type=jnp.float32)
        + down_bias.astype(jnp.float32)
    )
    outputs = result.astype(jnp.bfloat16).reshape(images, shard_len, model_width)
    backward_set = (gain_one, qkv_full, out_full, gain_two, up_full, down_full)
    norm_gain, qkv_back, out_back, mlp_gain, up_back, down_back = backward_set
    upstream = cotangent.reshape(images * shard_len, model_width)
    cot_rows = upstream.astype(jnp.float32)
    grad_down = outer_sum(activated, upstream)
    bias_down = jnp.sum(cot_rows, axis=0)
    d_preact = against(upstream, down_back) * gelu_slope(preact)
    grad_hidden = d_preact.astype(jnp.bfloat16)
    grad_up = outer_sum(hidden_two, grad_hidden)
    bias_up = jnp.sum(d_preact, axis=0)
    d_second = against(grad_hidden, up_back)
    second_gain = jnp.sum(d_second * normed_two, axis=0)
    second_shift = jnp.sum(d_second, axis=0)
    d_residual = cot_rows + norm_backward(d_second, normed_two, inv_two, mlp_gain)
    res_bf = d_residual.astype(jnp.bfloat16)
    grad_out = outer_sum(merged_rows, res_bf)
    bias_out = jnp.sum(d_residual, axis=0)
    d_merged = (
        against(res_bf, out_back).astype(jnp.bfloat16).reshape(images, shard_len, model_width)
    )
    d_heads = lax.all_to_all(d_merged, "seq", split_axis=2, concat_axis=1, tiled=True)
    split_grads = d_heads.reshape(images, seq_len, heads_local, HD)

    def backward_one(element):
        packed, live_count, attended_one, total_one, grad_one = element
        d_queries, d_keys, d_values = attend_backward(
            packed[:, 0],
            packed[:, 1],
            packed[:, 2],
            attended_one,
            total_one,
            grad_one,
            live_count,
            factor,
        )
        return jnp.stack([d_queries, d_keys, d_values], axis=1)

    grads_heads = lax.map(backward_one, (split_heads, valid_len, attended, log_totals, split_grads))
    d_tokens = lax.all_to_all(
        grads_heads.reshape(images, seq_len, 3, local_width),
        "seq",
        split_axis=1,
        concat_axis=3,
        tiled=True,
    )
    d_proj = d_tokens.reshape(images * shard_len, 3 * model_width)
    grad_qkv = outer_sum(hidden_one, d_proj)
    summed = jnp.sum(d_proj.astype(jnp.float32), axis=0)
    bias_qv = jnp.concatenate([summed[:model_width], summed[2 * model_width :]])
    d_first = against(d_proj, qkv_back)
    first_gain = jnp.sum(d_first * normed_one, axis=0)
    first_shift = jnp.sum(d_first, axis=0)
    d_inputs = (
        (d_residual + norm_backward(d_first, normed_one, inv_one, norm_gain))
        .astype(jnp.bfloat16)
        .reshape(images, shard_len, model_width)
    )
    partial_grads = (
        lax.psum_scatter(first_gain, "dp", scatter_dimension=0, tiled=True),
        lax.psum_scatter(first_shift, "dp", scatter_dimension=0, tiled=True),
        lax.psum_scatter(grad_qkv, "dp", scatter_dimension=0, tiled=True),
        lax.psum_scatter(bias_qv, "dp", scatter_dimension=0, tiled=True),
        lax.psum_scatter(grad_out, "dp", scatter_dimension=0, tiled=True),
        lax.psum_scatter(bias_out, "dp", scatter_dimension=0, tiled=True),
        lax.psum_scatter(second_gain, "dp", scatter_dimension=0, tiled=True),
        lax.psum_scatter(second_shift, "dp", scatter_dimension=0, tiled=True),
        lax.psum_scatter(grad_up, "dp", scatter_dimension=0, tiled=True),
        lax.psum_scatter(bias_up, "dp", scatter_dimension=0, tiled=True),
        lax.psum_scatter(grad_down, "dp", scatter_dimension=0, tiled=True),
        lax.psum_scatter(bias_down, "dp", scatter_dimension=0, tiled=True),
    )
    owned_grads = lax.psum(
        (
            partial_grads[0],
            partial_grads[1],
            partial_grads[2],
            partial_grads[3],
            partial_grads[4],
            partial_grads[5],
            partial_grads[6],
            partial_grads[7],
            partial_grads[8],
            partial_grads[9],
            partial_grads[10],
            partial_grads[11],
        ),
        "seq",
    )
    return (
        outputs,
        d_inputs,
        owned_grads[0],
        owned_grads[1],
        owned_grads[2],
        owned_grads[3],
        owned_grads[4],
        owned_grads[5],
        owned_grads[6],
        owned_grads[7],
        owned_grads[8],
        owned_grads[9],
        owned_grads[10],
        owned_grads[11],
    )


def solution(mesh):
    placed = (
        P("dp", "seq", None),
        P("dp", "seq", None),
        P("dp"),
        P("dp"),
        P("dp"),
        P("dp", None),
        P("dp"),
        P("dp", None),
        P("dp"),
        P("dp"),
        P("dp"),
        P("dp", None),
        P("dp"),
        P("dp", None),
        P("dp"),
    )
    return jax.shard_map(
        shards,
        mesh=mesh,
        in_specs=placed,
        out_specs=(
            P("dp", "seq", None),
            P("dp", "seq", None),
            P("dp"),
            P("dp"),
            P("dp", None),
            P("dp"),
            P("dp", None),
            P("dp"),
            P("dp"),
            P("dp"),
            P("dp", None),
            P("dp"),
            P("dp", None),
            P("dp"),
        ),
        check_vma=False,
    )
```

profile of v0, /device:TPU:0, one launch (start us, length us, event | category | flops | bytes accessed | tf_op | source)
XLA Modules:
  0.0 1005.6 jit_solution(9983935988012539980)
XLA Ops:
  10.0 10.3 %all-gather.2 = bf16[8,1,256]{2,1,0:T(2,128)(2,1)S(1)} all-gather(bf16[1,1,256]{2,1,0:T(2,128)(2,1)S(1)} %reshape.196), channel_id=1, replica_groups=mesh['dp'=8,'seq'=4] {'dp'}, dimensions={0}, use_global_device_ids=true | all-gather | bytes 4608 | tf_op jit(solution)/shard_map/all_gather | solution.py:117
  20.4 8.7 all-gather.1
  29.2 7.8 all-gather
  37.5 20.7 %all-gather.13.cloned.1.call-done = bf16[1024,3072]{1,0:T(8,128)(2,1)} async-done(((bf16[128,3072]{1,0:T(8,128)(2,1)}), bf16[1024,3072]{1,0:T(8,128)(2,1)}) %all-gather.13.cloned.1.call-update) | async-done | bytes 6291472 | tf_op jit(solution)/shard_map/all_gather | solution.py:116
  58.2 6.0 fusion.8
  64.2 4.6 reshape.184
  68.8 4.7 copy.85
  73.5 5.1 all-to-all-start
  79.3 70.4 %all-to-all-done = bf16[1,260,3,1024]{1,2,0,3:T(4,128)(2,1)S(1)} async-done(((bf16[1,260,3,1024]{1,2,0,3:T(4,128)(2,1)}), bf16[1,260,3,1024]{1,2,0,3:T(4,128)(2,1)S(1)}, u32[]{:S(2)}, u32[]{:S(2)}) %all-to-all-start) | async-done | bytes 1597472 | tf_op jit(solution)/shard_map/all_to_all | solution.py:150
  149.7 4.0 copy.108
  153.7 5.3 copy.87
  159.0 3.7 squeeze.42
  162.7 8.4 fusion.60
  171.1 10.4 %exponential_reduce_fusion = f32[4,1040]{1,0:T(4,128)S(1)} fusion(f32[4,1040,1040]{1,2,0:T(8,128)} %get-tuple-element.88, f32[4,1040]{1,0:T(4,128)S(1)} %get-tuple-element.87), kind=kLoop, calls=%fused_computation.6 | loop fusion | flops 8648640 | bytes 17338880 | tf_op jit(solution)/shard_map/while/body/eval_jaxpr/reduce_sum | solution.py:64
  181.5 9.6 convolution_convert_fusion.3
  191.2 2.2 copy.89
  193.9 6.8 reduce.8
  201.6 3.5 all-to-all-start.1
  205.1 8.9 all-gather.3
  214.0 7.9 all-gather.6
  222.0 8.7 all-gather.5
  230.7 7.8 all-gather.4
  239.0 5.6 bitcast_reduce_fusion
  246.0 2.6 fusion.61
  249.0 8.1 convolution_add_fusion
  257.1 7.0 fusion.62
  264.2 2.8 multiply_reduce_fusion.1
  267.0 1.9 fusion.59
  269.7 2.9 copy.91
  272.6 7.4 reduce.9
  280.1 3.6 reshape.230
  283.7 5.0 all-to-all-start.2
  288.7 3.3 fusion.56
  292.1 11.9 %all-to-all-done.2 = bf16[4,2,33280]{2,1,0:T(2,128)(2,1)} async-done(((bf16[4,2,33280]{2,1,0:T(2,128)(2,1)}), bf16[4,2,33280]{2,1,0:T(2,128)(2,1)}, u32[]{:S(2)}, u32[]{:S(2)}) %all-to-all-start.2) | async-done | bytes 532512 | tf_op jit(solution)/shard_map/all_to_all | solution.py:210
  304.0 4.7 reshape.231
  308.7 3.5 copy.92
  313.3 2.2 copy.93
  315.5 1.9 squeeze.47
  317.4 10.4 %convolution_convert_fusion = bf16[4,64,1040]{2,1,0:T(8,128)(2,1)} fusion(bf16[1040,4,64]{0,2,1:T(8,128)(2,1)S(1)} %squeeze.47, f32[4,1040,1040]{1,2,0:T(8,128)} %get-tuple-element.88, f32[4,1040]{1,0:T(4,128)S(1)} %log_add_fusion), kind=kOutput, calls=%fused_computation.20 | convolution fusion | flops 562698240 | bytes 18387200 | tf_op jit(solution)/shard_map/while/body/eval_jaxpr/hqk,qhe->khe/dot_general | solution.py:74
  327.8 3.7 copy.100
  332.7 11.3 %fusion.2 = bf16[4,1040,1040]{1,2,0:T(8,128)(2,1)} fusion(bf16[1040,4,64]{0,2,1:T(8,128)(2,1)S(1)} %squeeze.47, f32[4,1040,1040]{1,2,0:T(8,128)} %get-tuple-element.88, f32[4,1040]{1,0:T(4,128)S(1)} %bitcast.183, f32[4,1040]{1,0:T(4,128)S(1)} %log_add_fusion, bf16[1040,3,4,64]{0,3,2,1:T(8,128)(2,1)S(1)} %squeeze.42), kind=kOutput, calls=%fused_computation.4 | convolution fusion | flops 575411200 | bytes 27174912 | tf_op jit(solution)/shard_map/while/body/eval_jaxpr/qhe,khe->hqk/dot_general | solution.py:77
  344.0 6.8 convolution_convert_fusion.1
  350.8 2.2 copy.99
  353.0 6.3 convolution_convert_fusion.2
  359.3 3.4 copy.98
  362.8 5.0 pad_maximum_fusion
  367.8 51.5 %all_to_all.60 = bf16[1,1040,3,256]{3,2,0,1:T(4,128)(2,1)S(1)} all-to-all(bf16[1,1040,3,256]{3,2,0,1:T(4,128)(2,1)S(1)} %pad_maximum_fusion), channel_id=1, replica_groups=mesh['dp'=8,'seq'=4] {'seq'}, dimensions={1} | all-to-all | bytes 3194880 | tf_op jit(solution)/shard_map/all_to_all | solution.py:228
  419.7 1.8 copy.102
  421.5 4.2 reshape.190
  425.6 8.0 fusion.41
  434.9 13.9 %fusion.36 = f32[1024,4096]{1,0:T(8,128)} fusion(bf16[260,4096]{1,0:T(8,128)(2,1)} %copy-done.11, f32[260,1024]{1,0:T(8,128)S(1)} %copy-done.1, f32[1024]{0:T(1024)S(1)} %bitcast.176, f32[1024]{0:T(1024)S(1)} %bitcast.174, f32[260]{0:T(512)S(1)} %add_rsqrt_fusion, f32[260]{0:T(512)S(1)} %broadcast_multiply_fusion.4), kind=kOutput, calls=%fused_computation.62 | convolution fusion | flops 2182369280 | bytes 19982368 | tf_op jit(solution)/shard_map/dot_general | solution.py:50
  449.9 13.7 %fusion.45 = f32[4096,1024]{1,0:T(8,128)} fusion(bf16[1,260,1024]{2,1,0:T(8,128)(2,1)S(1)} %copy-done.9, f32[260,4096]{1,0:T(8,128)} %convolution_add_fusion), kind=kOutput, calls=%fused_computation.77 | convolution fusion | flops 2186362880 | bytes 21569536 | tf_op jit(solution)/shard_map/dot_general | solution.py:50
  463.6 60.8 %reduce-scatter.5.cloned.1.call-done = f32[128,3072]{1,0:T(8,128)} async-done(((f32[1024,3072]{1,0:T(8,128)}), f32[128,3072]{1,0:T(8,128)}) %reduce-scatter.5.cloned.1.call-update) | async-done | bytes 1572880 | tf_op jit(solution)/shard_map/reduce_scatter | solution.py:250
  524.4 120.0 %reduce-scatter.9.cloned.1.call-done = f32[128,4096]{1,0:T(8,128)} async-done(((f32[1024,4096]{1,0:T(8,128)}), f32[128,4096]{1,0:T(8,128)}) %reduce-scatter.9.cloned.1.call-update) | async-done | bytes 2097168 | tf_op jit(solution)/shard_map/reduce_scatter | solution.py:256
  644.4 120.0 %reduce-scatter.11.cloned.1.call-done = f32[512,1024]{1,0:T(8,128)} async-done(((f32[4096,1024]{1,0:T(8,128)}), f32[512,1024]{1,0:T(8,128)}) %reduce-scatter.11.cloned.1.call-update) | async-done | bytes 2097168 | tf_op jit(solution)/shard_map/reduce_scatter | solution.py:258
  765.0 8.6 all-gather.7
  776.1 8.0 fusion.22
  784.2 5.4 fusion.30
  789.5 25.7 %all-reduce.8 = (f32[1024]{0:T(1024)S(1)}, f32[1024]{0:T(1024)S(1)}, f32[2048]{0:T(1024)S(1)}, f32[1024]{0:T(1024)S(1)}, f32[1024]{0:T(1024)S(1)}, /*index=5*/f3...) all-reduce(f32[1024]{0:T(1024)S(1)} %get-tuple-element.52, ...), channel_id=2, replica_groups=mesh['dp'=8,'seq'=4] {'dp'}, use_global_device_ids=true, to_apply=%region_12.13.clone | all-reduce | flops 12288 | bytes 98304
  815.8 15.4 %all-reduce.9 = (f32[128]{0:T(128)}, f32[128]{0:T(128)}, f32[256]{0:T(256)}, f32[128]{0:T(128)}, f32[128]{0:T(128)}, /*index=5*/f32[128]{0:T(128)}, f32[512]{0:T(512)}, f32[128]{0:T(128)}) all-reduce(f32[128]{0:T(128)S(1)} %dynamic-slice.3, f32[128]{0:T(128)S(1)} %dynamic-slice.5, ...), channel_id=1, replica_groups=mesh['dp'=8,'seq'=4] {'seq'}, use_global_device_ids=true, to_apply=%region_13.14 | all-reduce | flops 1536 | bytes 12288 | tf_op jit(solution)/shard_map/psum | solution.py:261
  832.5 159.1 %all-reduce.13.cloned.1.call-done = (f32[128,3072]{1,0:T(8,128)}, f32[128,1024]{1,0:T(8,128)}, f32[128,4096]{1,0:T(8,128)}, f32[512,1024]{1,0:T(8,128)}) async-done(((f32[128,3072]{1,0:T(8,128)}, f32[128,1024]{1,0:T(8,128)}, f32[128,4096]{1,0:T(8,128)}, f32[512,1024]{1,0:T(8,128)}), (f32[128,3072]{1,0:T(8,128)}, f32[128,1024]{1,0:T(8,128)}, f32[128,4096]{1,0:T(8,128)}, ...) | async-done | bytes 6291472 | tf_op jit(solution)/shard_map/psum | solution.py:261
  991.5 2.9 copy.125
  995.2 1.3 copy.127
  997.5 1.3 copy.128
  (127 shorter events, 18.0 us)
Async XLA Ops:
  7.2 2.8 copy-start.24
  7.2 13.3 %copy-start.17 = (bf16[128]{0:T(256)(128)(2,1)S(1)}, bf16[128]{0:T(256)(128)(2,1)}, u32[]{:S(2)}) copy-start(bf16[128]{0:T(256)(128)(2,1)} %param.19) | copy-start | bytes 772
  7.2 22.0 %copy-start.18 = (bf16[128]{0:T(256)(128)(2,1)S(1)}, bf16[128]{0:T(256)(128)(2,1)}, u32[]{:S(2)}) copy-start(bf16[128]{0:T(256)(128)(2,1)} %param.18) | copy-start | bytes 772
  7.2 29.8 %copy-start.2 = (bf16[1,260,1024]{2,1,0:T(8,128)(2,1)S(1)}, bf16[1,260,1024]{2,1,0:T(8,128)(2,1)}, u32[]{:S(2)}) copy-start(bf16[1,260,1024]{2,1,0:T(8,128)(2,1)} %param.15) | copy-start | bytes 1597444
  7.2 51.0 %all-gather.13.cloned.1.call-start = ((), (), s32[]{:S(2)}) async-start(), calls=%async_computation.8 | async-start | bytes 7077888 | tf_op jit(solution)/shard_map/all_gather | solution.py:116
  8.0 238.1 %all-gather.15.cloned.1.call-start = ((), (), s32[]{:S(2)}) async-start(), calls=%async_computation.9 | async-start | bytes 2359296 | tf_op jit(solution)/shard_map/all_gather | solution.py:118
  8.7 240.3 %all-gather.17.cloned.1.call-start = ((), (), s32[]{:S(2)}) async-start(), calls=%async_computation.10 | async-start | bytes 9437184 | tf_op jit(solution)/shard_map/all_gather | solution.py:122
  9.4 247.7 %all-gather.19.cloned.1.call-start = ((), (), s32[]{:S(2)}) async-start(), calls=%async_computation.11 | async-start | bytes 9437184 | tf_op jit(solution)/shard_map/all_gather | solution.py:124
  73.5 76.2 %all-to-all-start = ((bf16[1,260,3,1024]{1,2,0,3:T(4,128)(2,1)}), bf16[1,260,3,1024]{1,2,0,3:T(4,128)(2,1)S(1)}, u32[]{:S(2)}, u32[]{:S(2)}) async-start(bf16[1,260,3,1024]{1,2,0,3:T(4,128)(2,1)} %copy.85), calls=%async_computation | async-start | bytes 6291456 | tf_op jit(solution)/shard_map/all_to_all | solution.py:150
  191.2 10.5 %copy-start.6 = (bf16[4,64,1040]{2,1,0:T(8,128)(2,1)}, bf16[4,64,1040]{2,1,0:T(8,128)(2,1)S(1)}, u32[]{:S(2)}) copy-start(bf16[4,64,1040]{2,1,0:T(8,128)(2,1)S(1)} %convolution_convert_fusion.3) | copy-start | bytes 1597444
  193.9 11.2 %copy-start.19 = (bf16[128]{0:T(256)(128)(2,1)S(1)}, bf16[128]{0:T(256)(128)(2,1)}, u32[]{:S(2)}) copy-start(bf16[128]{0:T(256)(128)(2,1)} %param.23) | copy-start | bytes 772
  193.9 20.1 %copy-start.16 = (bf16[512]{0:T(512)(128)(2,1)S(1)}, bf16[512]{0:T(512)(128)(2,1)}, u32[]{:S(2)}) copy-start(bf16[512]{0:T(512)(128)(2,1)} %param.27) | copy-start | bytes 3076
  193.9 28.1 %copy-start.20 = (bf16[128]{0:T(256)(128)(2,1)S(1)}, bf16[128]{0:T(256)(128)(2,1)}, u32[]{:S(2)}) copy-start(bf16[128]{0:T(256)(128)(2,1)} %param.25) | copy-start | bytes 772
  193.9 36.8 %copy-start.21 = (bf16[128]{0:T(256)(128)(2,1)S(1)}, bf16[128]{0:T(256)(128)(2,1)}, u32[]{:S(2)}) copy-start(bf16[128]{0:T(256)(128)(2,1)} %param.24) | copy-start | bytes 772
  201.6 36.9 %all-to-all-start.1 = ((bf16[4,2,33280]{2,1,0:T(2,128)(2,1)}), bf16[4,2,33280]{2,1,0:T(2,128)(2,1)S(1)}, u32[]{:S(2)}, u32[]{:S(2)}) async-start(bf16[4,2,33280]{2,1,0:T(2,128)(2,1)} %reshape.228), calls=%async_computation.1 | async-start | bytes 1064960 | tf_op jit(solution)/shard_map/all_to_all | solution.py:165
  244.7 1.3 copy-start.3
  248.7 15.5 %copy-start = (f32[260,1024]{1,0:T(8,128)}, f32[260,1024]{1,0:T(8,128)S(1)}, u32[]{:S(2)}) copy-start(f32[260,1024]{1,0:T(8,128)S(1)} %get-tuple-element.90) | copy-start | bytes 3194884
  249.0 8.1 copy-start.8
  257.1 7.1 copy-start.23
  264.1 2.9 copy-start.11
  267.0 1.9 copy-start.12
  280.1 8.7 copy-start.10
  283.7 20.3 %all-to-all-start.2 = ((bf16[4,2,33280]{2,1,0:T(2,128)(2,1)}), bf16[4,2,33280]{2,1,0:T(2,128)(2,1)}, u32[]{:S(2)}, u32[]{:S(2)}) async-start(bf16[4,2,33280]{2,1,0:T(2,128)(2,1)} %reshape.230), calls=%async_computation.2 | async-start | bytes 1064960 | tf_op jit(solution)/shard_map/all_to_all | solution.py:210
  288.7 174.9 %reduce-scatter.7.cloned.1.call-start = ((), (), s32[]{:S(2)}) async-start(), calls=%async_computation.13 | async-start | bytes 4718592 | tf_op jit(solution)/shard_map/reduce_scatter | solution.py:252
  292.0 232.4 %reduce-scatter.5.cloned.1.call-start = ((), (), s32[]{:S(2)}) async-start(), calls=%async_computation.12 | async-start | bytes 14155776 | tf_op jit(solution)/shard_map/reduce_scatter | solution.py:250
  359.3 3.5 copy-start.7
  421.5 4.2 copy-start.4
  433.6 1.2 copy-start.1
  433.7 210.7 %reduce-scatter.9.cloned.1.call-start = ((), (), s32[]{:S(2)}) async-start(), calls=%async_computation.14 | async-start | bytes 18874368 | tf_op jit(solution)/shard_map/reduce_scatter | solution.py:256
  448.7 1.1 copy-start.9
  448.8 315.6 %reduce-scatter.11.cloned.1.call-start = ((), (), s32[]{:S(2)}) async-start(), calls=%async_computation.15 | async-start | bytes 18874368 | tf_op jit(solution)/shard_map/reduce_scatter | solution.py:258
  463.6 528.0 %all-reduce.13.cloned.1.call-start = ((), (), s32[]{:S(2)}) async-start(), calls=%async_computation.16 | async-start | bytes 12582912 | tf_op jit(solution)/shard_map/psum | solution.py:261
  764.3 0.7 copy-start.22
  764.3 9.2 copy-start.25
  776.1 8.1 copy-start.5
  991.5 2.9 copy-start.15
  991.5 3.7 copy-start.14
  995.2 2.3 copy-start.13
Sparse Core Ops, SparseCore 0:
  9.9 48.2 all-gather.12
  60.1 27.8 all-gather.14
  89.9 54.3 all-gather.16
  146.1 54.3 all-gather.18
  292.6 51.8 reduce-scatter.6
  433.8 90.5 reduce-scatter.4
  528.4 115.9 reduce-scatter.8
  648.3 115.9 reduce-scatter.10
  767.1 224.3 all-reduce.12
where the time goes:
time: 1010 us
  waiting for transfers between devices  565 us (56%)
  blocking collectives  161 us (16%)
  matrix products  132 us (13%)
  local copies, waits for them, and re-layouts  79.9 us (8%)
  other arithmetic  35.3 us (3%)
  between operations  17.1 us (2%)
  starting transfers between devices  14.2 us (1%)
    psum x1, waiting for transfers between devices, shards(): lax.psum((partial_grads[0], partial_grads[1], partial_grads[2], partial_g...  159 us
    reduce_scatter x1, waiting for transfers between devices, shards(): lax.psum_scatter(grad_up, 'dp', scatter_dimension=0, tiled=True)  120 us
    reduce_scatter x1, waiting for transfers between devices, shards(): lax.psum_scatter(grad_down, 'dp', scatter_dimension=0, tiled=True)  120 us
    all_to_all x1, waiting for transfers between devices, shards(): lax.all_to_all(projected.reshape(images, shard_len, 3, model_width), 'seq...  70.4 us
    reduce_scatter x1, waiting for transfers between devices, shards(): lax.psum_scatter(grad_qkv, 'dp', scatter_dimension=0, tiled=True)  60.8 us
    all_to_all x1, blocking collectives, shards(): lax.all_to_all(grads_heads.reshape(images, seq_len, 3, local_width), 'seq...  51.5 us
    dot_general x4, matrix products, outer_sum(): lax.dot_general(left_mat, right_mat, (((0,), (0,)), ((), ())), preferred_...  38.8 us
    unnamed x1, blocking collectives  25.7 us
  transfers between devices with their start and end apart: 12, of which 7 were waited for; matrix products, arithmetic and copies ran while one was open for 21% of the time, Pallas kernels for 0%

commit v1 on v0

v1 whole, which is shorter than its diff:
```python
import math

import jax
import jax.numpy as jnp
from jax import lax
from jax.sharding import PartitionSpec as P

HD = 64


EPSILON = 1e-05
ROOT_HALF = 0.7071067811865476
GAUSS_DENSITY = 0.3989422804014327
NEG_LARGE = -1e30


def norm_forward(values, gain_vec, shift_vec):
    mean_val = jnp.mean(values, axis=-1, keepdims=True)
    centred = values - mean_val
    inv_std = lax.rsqrt(jnp.mean(centred * centred, axis=-1, keepdims=True) + EPSILON)
    normed = centred * inv_std
    return (normed, inv_std, normed * gain_vec.astype(jnp.float32) + shift_vec.astype(jnp.float32))


def norm_backward(upstream, normed, inv_std, gain_vec):
    scaled = upstream * gain_vec.astype(jnp.float32)
    first_mean = jnp.mean(scaled, axis=-1, keepdims=True)
    second_mean = jnp.mean(scaled * normed, axis=-1, keepdims=True)
    return inv_std * (scaled - first_mean - normed * second_mean)


def gelu_value(preact):
    return 0.5 * preact * (1.0 + lax.erf(preact * ROOT_HALF))


def gelu_slope(preact):
    return (
        0.5 * (1.0 + lax.erf(preact * ROOT_HALF))
        + preact * jnp.exp(-0.5 * preact * preact) * GAUSS_DENSITY
    )


def against(left_mat, right_mat):
    return lax.dot_general(
        left_mat, right_mat, (((1,), (1,)), ((), ())), preferred_element_type=jnp.float32
    )


def outer_sum(left_mat, right_mat):
    return lax.dot_general(
        left_mat, right_mat, (((0,), (0,)), ((), ())), preferred_element_type=jnp.float32
    )


def scores_of(queries, keys, valid_count, factor):
    logits = jnp.einsum("qhe,khe->hqk", queries, keys, preferred_element_type=jnp.float32) * factor
    key_live = lax.iota(jnp.int32, keys.shape[0]) < valid_count
    return jnp.where(key_live[None, None, :], logits, NEG_LARGE)


def attend_forward(queries, keys, values_in, valid_count, factor):
    logits = scores_of(queries, keys, valid_count, factor)
    row_max = jnp.max(logits, axis=-1, keepdims=True)
    log_total = row_max + jnp.log(jnp.sum(jnp.exp(logits - row_max), axis=-1, keepdims=True))
    weights = jnp.exp(logits - log_total).astype(jnp.bfloat16)
    output = jnp.einsum("hqk,khe->qhe", weights, values_in, preferred_element_type=jnp.float32)
    return (output.astype(jnp.bfloat16), log_total)


def attend_backward(queries, keys, values_in, output, log_total, d_output, valid_count, factor):
    logits = scores_of(queries, keys, valid_count, factor)
    attn_probs = jnp.exp(logits - log_total)
    probs_bf = attn_probs.astype(jnp.bfloat16)
    d_values = jnp.einsum(
        "hqk,qhe->khe", probs_bf, d_output, preferred_element_type=jnp.float32
    ).astype(jnp.bfloat16)
    d_probs = jnp.einsum("qhe,khe->hqk", d_output, values_in, preferred_element_type=jnp.float32)
    row_dot = jnp.sum(d_output.astype(jnp.float32) * output.astype(jnp.float32), axis=-1)
    d_logits = (factor * attn_probs * (d_probs - jnp.transpose(row_dot)[:, :, None])).astype(
        jnp.bfloat16
    )
    d_queries = jnp.einsum(
        "hqk,khe->qhe", d_logits, keys, preferred_element_type=jnp.float32
    ).astype(jnp.bfloat16)
    d_keys = jnp.einsum(
        "hqk,qhe->khe", d_logits, queries, preferred_element_type=jnp.float32
    ).astype(jnp.bfloat16)
    return (d_queries, d_keys, d_values)


def seq_total(part):
    share = lax.psum_scatter(part, "seq", scatter_dimension=0, tiled=True)
    return lax.all_gather(share, "seq", axis=0, tiled=True).astype(jnp.float32)


def attention_forward(projected, valid_len, images, factor):
    local_width = projected.shape[1] // 3
    heads = local_width // HD
    packed = projected.reshape(images, -1, 3, heads, HD)

    def one(element):
        rows, live = element
        return attend_forward(rows[:, 0], rows[:, 1], rows[:, 2], live, factor)

    attended, totals = lax.map(one, (packed, valid_len))
    return attended.reshape(-1, local_width), totals


def attention_backward(projected, valid_len, attended, saved, d_heads, images, factor):
    local_width = projected.shape[1] // 3
    heads = local_width // HD
    packed = projected.reshape(images, -1, 3, heads, HD)

    def one(element):
        rows, live, out, total, grad = element
        return jnp.stack(
            attend_backward(
                rows[:, 0], rows[:, 1], rows[:, 2], out, total, grad, live, factor
            ),
            axis=1,
        )

    shape = (images, packed.shape[1], heads, HD)
    grads = lax.map(
        one, (packed, valid_len, attended.reshape(shape), saved, d_heads.reshape(shape))
    )
    return grads.reshape(-1, 3 * local_width)


def shards(
    inputs,
    cotangent,
    valid_len,
    ln1_gain,
    ln1_bias,
    w_qkv,
    b_qv,
    w_out,
    b_out,
    ln2_gain,
    ln2_bias,
    w_up,
    b_up,
    w_down,
    b_down,
):
    images, shard_len, width = inputs.shape
    groups = lax.axis_size("seq")
    owners = lax.axis_size("dp")
    my_seq = lax.axis_index("seq")
    my_dp = lax.axis_index("dp")
    local_width = width // groups
    heads_local = local_width // HD
    rows_owned = w_qkv.shape[0]
    hidden_local = w_down.shape[0]
    hidden_all = hidden_local * owners
    tokens = images * shard_len
    factor = 1.0 / math.sqrt(HD)
    bf16, f32 = jnp.bfloat16, jnp.float32

    tokens_all = lax.all_gather(inputs, "seq", axis=1, tiled=True)
    qkv_slice = lax.dynamic_slice_in_dim(
        w_qkv.reshape(rows_owned, 3, groups, local_width), my_seq, 1, axis=2
    ).reshape(rows_owned, 3 * local_width)
    qkv_cols = lax.all_gather(qkv_slice, "dp", axis=0, tiled=True)
    vectors = (ln1_gain, ln1_bias, b_out, ln2_gain, ln2_bias, b_down, b_qv)
    packed = lax.all_gather(jnp.concatenate(vectors), "dp", axis=0, tiled=False)
    pieces = []
    offset = 0
    for vec in vectors:
        pieces.append(packed[:, offset : offset + vec.shape[0]].reshape(-1))
        offset += vec.shape[0]
    gain_one, bias_one, out_bias, gain_two, bias_two, down_bias, qv_bias = pieces
    out_full = lax.all_gather(w_out, "dp", axis=0, tiled=True)
    up_cols = lax.all_to_all(w_up, "dp", split_axis=1, concat_axis=0, tiled=True)
    cot_all = lax.all_gather(
        cotangent.reshape(tokens, width), "dp", axis=0, tiled=True
    )

    seq_len = tokens_all.shape[1]
    rows_all = tokens_all.reshape(images * seq_len, width)
    hidden_one = norm_forward(rows_all.astype(f32), gain_one, bias_one)[2].astype(bf16)
    qkv_bias = jnp.concatenate(
        [qv_bias[:width], jnp.zeros((width,), bf16), qv_bias[width:]]
    ).reshape(3, groups, local_width)
    qkv_bias = lax.dynamic_slice_in_dim(qkv_bias, my_seq, 1, axis=1).reshape(-1).astype(f32)
    projected = (
        jnp.dot(hidden_one, qkv_cols, preferred_element_type=f32) + qkv_bias
    ).astype(bf16)
    attended, saved = attention_forward(projected, valid_len, images, factor)
    merged = lax.all_to_all(
        attended.reshape(images, seq_len, local_width),
        "seq",
        split_axis=1,
        concat_axis=2,
        tiled=True,
    )
    merged_rows = merged.reshape(tokens, width)
    token_rows = inputs.reshape(tokens, width).astype(f32)
    residual = (
        token_rows
        + jnp.dot(merged_rows, out_full, preferred_element_type=f32)
        + out_bias.astype(f32)
    )
    normed_two, inv_two, pre_two = norm_forward(residual, gain_two, bias_two)

    hidden_two = lax.all_gather(pre_two.astype(bf16), "dp", axis=0, tiled=True)
    d_act = against(cot_all, w_down)
    preact = jnp.dot(hidden_two, up_cols, preferred_element_type=f32) + b_up.astype(f32)
    activated = gelu_value(preact).astype(bf16)
    d_preact = d_act * gelu_slope(preact)
    grad_hidden = d_preact.astype(bf16)
    d_second = lax.psum_scatter(
        against(grad_hidden, up_cols).astype(bf16), "dp", scatter_dimension=0, tiled=True
    ).astype(f32)
    mlp_part = jnp.dot(activated, w_down, preferred_element_type=f32).astype(bf16)
    mlp_sum = lax.psum_scatter(mlp_part, "dp", scatter_dimension=0, tiled=True).astype(f32)
    outputs = (residual + mlp_sum + down_bias.astype(f32)).astype(bf16)
    outputs = outputs.reshape(images, shard_len, width)
    grad_down = seq_total(outer_sum(activated, cot_all).astype(bf16))
    grad_up = lax.all_to_all(
        outer_sum(hidden_two, grad_hidden).astype(bf16),
        "dp",
        split_axis=0,
        concat_axis=1,
        tiled=True,
    )
    grad_up = seq_total(grad_up)
    bias_up = jnp.sum(d_preact, axis=0)

    cot_rows = cotangent.reshape(tokens, width).astype(f32)
    bias_down = jnp.sum(cot_rows, axis=0)
    second_gain = jnp.sum(d_second * normed_two, axis=0)
    second_shift = jnp.sum(d_second, axis=0)
    d_residual = cot_rows + norm_backward(d_second, normed_two, inv_two, gain_two)
    res_bf = d_residual.astype(bf16)
    d_merged = against(res_bf, out_full).astype(bf16).reshape(images, shard_len, width)
    d_heads = lax.all_to_all(d_merged, "seq", split_axis=2, concat_axis=1, tiled=True)
    bias_out = jnp.sum(d_residual, axis=0)
    grad_out = lax.psum_scatter(
        outer_sum(merged_rows, res_bf).astype(bf16), "dp", scatter_dimension=0, tiled=True
    )
    grad_out = seq_total(grad_out)

    d_proj = attention_backward(
        projected,
        valid_len,
        attended,
        saved,
        d_heads.reshape(images * seq_len, local_width),
        images,
        factor,
    )
    d_first = lax.psum_scatter(
        against(d_proj, qkv_cols).astype(bf16).reshape(images, seq_len, width),
        "seq",
        scatter_dimension=1,
        tiled=True,
    )
    d_first = d_first.reshape(tokens, width).astype(f32)
    grad_qkv = lax.psum_scatter(
        outer_sum(hidden_one, d_proj).astype(bf16), "dp", scatter_dimension=0, tiled=True
    )
    grad_qkv = lax.all_gather(grad_qkv, "seq", axis=0, tiled=False)
    grad_qkv = (
        grad_qkv.reshape(groups, rows_owned, 3, local_width)
        .transpose(1, 2, 0, 3)
        .reshape(rows_owned, 3 * width)
        .astype(f32)
    )
    summed = jnp.sum(d_proj.astype(f32), axis=0).reshape(3, 1, local_width)
    bias_qv = lax.dynamic_update_slice(
        jnp.zeros((2, groups, local_width), f32),
        jnp.concatenate([summed[:1], summed[2:]], axis=0),
        (0, my_seq, 0),
    ).reshape(-1)
    normed_one, inv_one, _ = norm_forward(token_rows, gain_one, bias_one)
    first_gain = jnp.sum(d_first * normed_one, axis=0)
    first_shift = jnp.sum(d_first, axis=0)
    d_inputs = (
        (d_residual + norm_backward(d_first, normed_one, inv_one, gain_one))
        .astype(bf16)
        .reshape(images, shard_len, width)
    )

    def owned(*parts):
        sums = lax.psum(jnp.concatenate(parts), ("dp", "seq"))
        result = []
        start = 0
        for part in parts:
            share = part.shape[0] // owners
            result.append(lax.dynamic_slice_in_dim(sums, start + my_dp * share, share))
            start += part.shape[0]
        return result

    own_second_gain, own_second_shift, own_out, own_down = owned(
        second_gain, second_shift, bias_out, bias_down
    )
    own_up = lax.psum(bias_up, "seq")
    own_gain, own_shift, own_qv = owned(first_gain, first_shift, bias_qv)
    return (
        outputs,
        d_inputs,
        own_gain,
        own_shift,
        grad_qkv,
        own_qv,
        grad_out,
        own_out,
        own_second_gain,
        own_second_shift,
        grad_up,
        own_up,
        grad_down,
        own_down,
    )


def solution(mesh):
    placed = (
        P("dp", "seq", None),
        P("dp", "seq", None),
        P("dp"),
        P("dp"),
        P("dp"),
        P("dp", None),
        P("dp"),
        P("dp", None),
        P("dp"),
        P("dp"),
        P("dp"),
        P("dp", None),
        P("dp"),
        P("dp", None),
        P("dp"),
    )
    return jax.shard_map(
        shards,
        mesh=mesh,
        in_specs=placed,
        out_specs=(
            P("dp", "seq", None),
            P("dp", "seq", None),
            P("dp"),
            P("dp"),
            P("dp", None),
            P("dp"),
            P("dp", None),
            P("dp"),
            P("dp"),
            P("dp"),
            P("dp", None),
            P("dp"),
            P("dp", None),
            P("dp"),
        ),
        check_vma=False,
    )
```

time: 1010 us -> 720 us (0.71)
  waiting for transfers between devices: 565 us -> 181 us
  blocking collectives: 161 us -> 257 us
  matrix products: 132 us -> 112 us
    reduce_scatter x4 -> x5, waiting for transfers between devices: 301 us -> 0.04 us  [the longest x3 0.04 us: seq_total(): share = lax.psum_scatter(part, 'seq', scatter_dimension=0, tiled=True)]
    psum x1 -> x0, waiting for transfers between devices: 159 us -> none  [shards(): lax.psum((partial_grads[0], partial_grads[1], partial_grads[2], partial_g...]
    all_gather x4 -> x7, waiting for transfers between devices: 20.7 us -> 152 us  [the longest x1 70.1 us: shards(): tokens_all = lax.all_gather(inputs, 'seq', axis=1, tiled=True)]
    unnamed x1 -> x2, blocking collectives: 25.7 us -> 129 us
    all_to_all x2, waiting for transfers between devices: 70.4 us -> 17.1 us  [the longest x1 17.1 us: shards(): lax.all_to_all(w_up, 'dp', split_axis=1, concat_axis=0, tiled=True)]
    psum x1 -> x2, blocking collectives: 15.4 us -> 52.5 us  [the longest x1 41.9 us: owned(): sums = lax.psum(jnp.concatenate(parts), ('dp', 'seq'))]
    all_to_all x1, blocking collectives: 51.5 us -> 20.1 us  [shards(): lax.all_to_all(attended.reshape(images, seq_len, local_width), 'seq', spl...]
    unnamed x79 -> x84, local copies, waits for them, and re-layouts: 22.7 us -> 43.7 us
  transfers between devices with their start and end apart: 12 -> 18, of which waited for: 7 -> 7; matrix products, arithmetic and copies ran while one was open for 21% -> 48% of each run, Pallas kernels for 0% -> 0%
where the time goes in v1:
time: 720 us; the launch traced here: 713 us
  blocking collectives  257 us (36%)
  waiting for transfers between devices  181 us (25%)
  matrix products  112 us (16%)
  local copies, waits for them, and re-layouts  81 us (11%)
  other arithmetic  44 us (6%)
  starting transfers between devices  21 us (3%)
  between operations  17.2 us (2%)
    unnamed x2, blocking collectives  129 us
    all_gather x1, waiting for transfers between devices, shards(): tokens_all = lax.all_gather(inputs, 'seq', axis=1, tiled=True)  70.1 us
    all_gather x1, waiting for transfers between devices, shards(): lax.all_gather(cotangent.reshape(tokens, width), 'dp', axis=0, tiled=True)  44.1 us
    unnamed x84, local copies, waits for them, and re-layouts  43.7 us
    psum x1, blocking collectives, owned(): sums = lax.psum(jnp.concatenate(parts), ('dp', 'seq'))  41.9 us
    all_gather x1, blocking collectives, shards(): grad_qkv = lax.all_gather(grad_qkv, 'seq', axis=0, tiled=False)  30 us
    all_gather x1, waiting for transfers between devices, shards(): qkv_cols = lax.all_gather(qkv_slice, 'dp', axis=0, tiled=True)  21.8 us
    dot_general x4, matrix products, outer_sum(): lax.dot_general(left_mat, right_mat, (((0,), (0,)), ((), ())), preferred_...  21.1 us
  transfers between devices with their start and end apart: 18, of which 7 were waited for; matrix products, arithmetic and copies ran while one was open for 48% of the time, Pallas kernels for 0%

profile of v1, /device:TPU:0, one launch (start us, length us, event | category | flops | bytes accessed | tf_op | source)
XLA Modules:
  0.0 713.0 jit_solution(1318024005570104675)
XLA Ops:
  7.3 3.0 copy.86
  13.7 10.3 %all-gather = bf16[8192]{0:T(1024)(128)(2,1)S(1)} all-gather(bf16[1024]{0:T(1024)(128)(2,1)S(1)} %dynamic-update-slice.6), channel_id=2, replica_groups=mesh['dp'=8,'seq'=4] {'dp'}, dimensions={0}, use_global_device_ids=true | all-gather | bytes 18432 | tf_op jit(solution)/shard_map/all_gather | solution.py:167
  24.9 70.1 %all-gather.12.cloned.1.call-done = bf16[1,1040,1024]{2,0,1:T(2,128)(2,1)} async-done(((bf16[1,260,1024]{2,0,1:T(2,128)(2,1)}), bf16[1,1040,1024]{2,0,1:T(2,128)(2,1)}) %all-gather.12.cloned.1.call-update) | async-done | bytes 2129936 | tf_op jit(solution)/shard_map/all_gather | solution.py:161
  95.0 3.0 convert_reduce_fusion
  100.1 21.8 %all-gather.14.cloned.1.call-done = bf16[1024,768]{0,1:T(8,128)(2,1)} async-done(((bf16[128,768]{0,1:T(8,128)(2,1)}), bf16[1024,768]{0,1:T(8,128)(2,1)}) %all-gather.14.cloned.1.call-update) | async-done | bytes 1572880 | tf_op jit(solution)/shard_map/all_gather | solution.py:165
  121.9 5.4 fusion.25
  127.2 2.9 copy.89
  130.1 8.4 %fusion.101 = (f32[4,1040]{1,0:T(4,128)S(1)}, f32[4,1040,1040]{1,2,0:T(8,128)}) fusion(bf16[1040,3,4,64]{0,3,2,1:T(8,128)(2,1)S(1)} %bitcast.240, pred[1040]{0:T(1024)(128)(4,1)S(1)} %iota_compare_fusion), kind=kOutput, calls=%fused_computation.157 | convolution fusion | flops 566754240 | bytes 18503936 | tf_op jit(solution)/shard_map/while/body/eval_jaxpr/qhe,khe->hqk/dot_general | solution.py:56
  138.5 9.4 %exponential_reduce_fusion = f32[4,1040]{1,0:T(4,128)S(1)} fusion(f32[4,1040,1040]{1,2,0:T(8,128)} %get-tuple-element.129, f32[4,1040]{1,0:T(4,128)S(1)} %get-tuple-element.128), kind=kLoop, calls=%fused_computation.6 | loop fusion | flops 8648640 | bytes 17338880 | tf_op jit(solution)/shard_map/while/body/eval_jaxpr/reduce_sum | solution.py:64
  147.9 10.5 %convolution_convert_fusion.6 = bf16[4,64,1040]{2,1,0:T(8,128)(2,1)} fusion(f32[4,1040,1040]{1,2,0:T(8,128)} %get-tuple-element.129, f32[4,1040]{1,0:T(4,128)S(1)} %log_add_fusion, bf16[1040,3,4,64]{0,3,2,1:T(8,128)(2,1)S(1)} %bitcast.241), kind=kOutput, calls=%fused_computation.44 | convolution fusion | flops 562698240 | bytes 18446336 | tf_op jit(solution)/shard_map/while/body/eval_jaxpr/hqk,khe->qhe/dot_general | solution.py:66
  158.4 3.7 copy.91
  162.5 6.7 reduce.9
  170.2 20.1 %all_to_all.68 = bf16[4,2,33280]{2,1,0:T(2,128)(2,1)S(1)} all-to-all(bf16[4,2,33280]{2,1,0:T(2,128)(2,1)} %reshape.292), channel_id=1, replica_groups=mesh['dp'=8,'seq'=4] {'seq'}, dimensions={0} | all-to-all | bytes 1064960 | tf_op jit(solution)/shard_map/all_to_all | solution.py:191
  192.0 7.4 %bitcast_reduce_fusion = bf16[1040,256]{1,0:T(8,128)(2,1)} fusion(bf16[1040,1,256]{2,1,0:T(2,128)(2,1)} %reshape.293), kind=kLoop, calls=%fused_computation.160 | loop fusion | bytes 1064960 | tf_op jit(solution)/shard_map/all_to_all | solution.py:191
  199.4 2.0 all_to_all.51
  203.8 2.6 fusion.102
  208.6 2.8 copy.95
  211.5 2.3 copy.93
  213.7 4.2 all-to-all-start.1
  218.0 17.1 %all-to-all-done.1 = bf16[128,8,512]{0,2,1:T(8,128)(2,1)} async-done(((bf16[128,8,512]{0,2,1:T(8,128)(2,1)}), bf16[128,8,512]{0,2,1:T(8,128)(2,1)}, u32[]{:S(2)}, u32[]{:S(2)}) %all-to-all-start.1) | async-done | bytes 1048608 | tf_op jit(solution)/shard_map/all_to_all | solution.py:175
  235.1 2.3 copy.94
  237.4 16.5 %all-gather.24.cloned.1.call-done = bf16[8,260,1024]{2,1,0:T(8,128)(2,1)} async-done(((bf16[1,260,1024]{2,1,0:T(8,128)(2,1)}), bf16[8,260,1024]{2,1,0:T(8,128)(2,1)}) %all-gather.24.cloned.1.call-update) | async-done | bytes 4259856 | tf_op jit(solution)/shard_map/all_gather | solution.py:207
  253.8 5.0 reshape.283
  258.8 8.2 %multiply_convert_fusion = (bf16[2080,512]{1,0:T(8,128)(2,1)}, f32[2080,512]{1,0:T(8,128)}) fusion(f32[512]{0:T(512)S(1)} %convert_element_type.251, bf16[2080,1024]{1,0:T(8,128)(2,1)} %reshape.283, bf16[1024,512]{1,0:T(8,128)(2,1)} %bitcast.260), kind=kOutput, calls=%fused_computation.34 | convolution fusion | flops 2187427840 | bytes 11700224 | tf_op jit(solution)/shard_map/dot_general | solution.py:209
  267.0 44.1 %all-gather.22.cloned.1.call-done = bf16[1,2080,1024]{2,0,1:T(2,128)(2,1)} async-done(((bf16[1,260,1024]{2,0,1:T(2,128)(2,1)}), bf16[1,2080,1024]{2,0,1:T(2,128)(2,1)}) %all-gather.22.cloned.1.call-update) | async-done | bytes 4259856 | tf_op jit(solution)/shard_map/all_gather | solution.py:176
  311.1 7.7 %fusion.51 = bf16[512,1024]{1,0:T(8,128)(2,1)} fusion(bf16[2080,512]{1,0:T(8,128)(2,1)} %get-tuple-element.132, bf16[1,2080,1024]{2,0,1:T(2,128)(2,1)} %all-gather.22.cloned.1.call-done), kind=kOutput, calls=%fused_computation.66 | convolution fusion | flops 2181562368 | bytes 7438336 | tf_op jit(solution)/shard_map/dot_general | solution.py:50
  318.9 6.1 convolution_convert_fusion.1
  325.1 4.5 fusion.103
  331.0 4.5 convolution_convert_fusion
  335.4 88.7 %fusion.95 = (bf16[264,1024]{1,0:T(8,128)(2,1)}, bf16[264,1024]{1,0:T(8,128)(2,1)S(1)}) fusion(bf16[2080,1024]{1,0:T(8,128)(2,1)} %convolution_convert_fusion.1, bf16[2080,1024]{1,0:T(8,128)(2,1)} %convolution_convert_fusion), kind=kCustom, calls=%all-reduce-scatter.3 | all-reduce-scatter fusion | flops 4325377 | bytes 9601536
  427.3 3.4 collective-permute-start
  432.0 4.3 concatenate.28
  436.3 4.3 concatenate.27
  440.6 2.0 fusion.79
  442.7 3.1 fusion.96
  446.8 2.6 convolution_convert_fusion.7
  449.5 2.7 fusion.67
  452.2 2.9 copy.96
  455.1 6.6 reduce.10
  461.7 2.3 reshape.294
  464.0 4.6 all-to-all-start.2
  468.6 6.8 convolution_convert_fusion.8
  475.4 8.1 %all-to-all-done.2 = bf16[4,2,33280]{2,1,0:T(2,128)(2,1)S(1)} async-done(((bf16[4,2,33280]{2,1,0:T(2,128)(2,1)}), bf16[4,2,33280]{2,1,0:T(2,128)(2,1)S(1)}, u32[]{:S(2)}, u32[]{:S(2)}) %all-to-all-start.2) | async-done | bytes 532512 | tf_op jit(solution)/shard_map/all_to_all | solution.py:238
  483.4 4.5 all-to-all-start.3
  488.0 2.9 reshape.295
  490.9 3.5 copy.97
  495.5 2.2 copy.98
  497.6 1.8 squeeze.47
  500.7 11.0 %fusion.5 = bf16[4,1040,1040]{1,2,0:T(8,128)(2,1)} fusion(bf16[1040,4,64]{0,2,1:T(8,128)(2,1)S(1)} %squeeze.47, f32[4,1040,1040]{1,2,0:T(8,128)} %get-tuple-element.129, f32[4,1040]{1,0:T(4,128)S(1)} %bitcast.266, f32[4,1040]{1,0:T(4,128)S(1)} %log_add_fusion, bf16[1040,3,4,64]{0,3,2,1:T(8,128)(2,1)S(1)} %bitcast.242), kind=kOutput, calls=%fused_computation.4 | convolution fusion | flops 575411200 | bytes 27174912 | tf_op jit(solution)/shard_map/while/body/eval_jaxpr/qhe,khe->hqk/dot_general | solution.py:77
  511.7 7.6 %fusion.30 = bf16[1040,1,4,64]{0,3,2,1:T(8,128)(2,1)} fusion(bf16[4,1040,1040]{1,2,0:T(8,128)(2,1)} %fusion.5, bf16[1040,3,4,64]{0,3,2,1:T(8,128)(2,1)S(1)} %bitcast.243), kind=kOutput, calls=%fused_computation.46 | convolution fusion | flops 554045440 | bytes 9775104 | tf_op jit(solution)/shard_map/while/body/eval_jaxpr/hqk,qhe->khe/dot_general | solution.py:85
  519.3 2.3 copy.116
  521.7 5.5 fusion.29
  527.2 9.6 %fusion.31 = bf16[1040,1,4,64]{0,3,2,1:T(8,128)(2,1)S(1)} fusion(bf16[1040,4,64]{0,2,1:T(8,128)(2,1)S(1)} %squeeze.47, f32[4,1040,1040]{1,2,0:T(8,128)} %get-tuple-element.129, f32[4,1040]{1,0:T(4,128)S(1)} %log_add_fusion), kind=kOutput, calls=%fused_computation.47 | convolution fusion | flops 562698240 | bytes 18387200 | tf_op jit(solution)/shard_map/while/body/eval_jaxpr/hqk,qhe->khe/dot_general | solution.py:74
  538.4 4.0 fusion.46
  544.9 10.6 %psum.23 = f32[512]{0:T(512)} all-reduce(f32[512]{0:T(512)S(1)} %get-tuple-element.134), channel_id=1, replica_groups=mesh['dp'=8,'seq'=4] {'seq'}, use_global_device_ids=true, to_apply=%region_30.31 | all-reduce | flops 512 | bytes 4096 | tf_op jit(solution)/shard_map/psum | solution.py:299
  555.6 4.7 fusion.26
  560.3 40.4 %fusion.2 = bf16[264,1024]{1,0:T(8,128)(2,1)S(1)} fusion(bf16[1,1040,1024]{2,1,0:T(8,128)(2,1)} %fusion.26), kind=kCustom, calls=%all-reduce-scatter.2 | all-reduce-scatter fusion | flops 1081345 | bytes 2671104
  601.0 2.5 collective-permute-start.2
  603.5 2.0 collective-permute-done.2
  607.0 41.9 %all-reduce.6 = (f32[4096]{0:T(1024)S(1)}, f32[4096]{0:T(1024)S(1)}) all-reduce(f32[4096]{0:T(1024)S(1)} %pad_maximum_fusion.1, f32[4096]{0:T(1024)S(1)} %pad_maximum_fusion.2), channel_id=1, replica_groups=mesh['dp'=8,'seq'=4] {'dp','seq'}, use_global_device_ids=true, to_apply=%region_19.20 | all-reduce | flops 8192 | bytes 65536 | tf_op jit(solution)/shard_map/psum | solution.py:287
  652.1 30.0 %all-gather.2 = bf16[512,768]{1,0:T(8,128)(2,1)S(1)} all-gather(bf16[128,768]{1,0:T(8,128)(2,1)} %reduce-scatter.13.cloned.1.call-done), channel_id=4, replica_groups=mesh['dp'=8,'seq'=4] {'seq'}, dimensions={0}, use_global_device_ids=true | all-gather | bytes 983040 | tf_op jit(solution)/shard_map/all_gather | solution.py:264
  684.7 2.9 convert_element_type.290
  687.6 14.5 %all_gather.45 = bf16[128,1024]{1,0:T(8,128)(2,1)S(1)} all-gather(bf16[32,1024]{1,0:T(8,128)(2,1)} %reduce-scatter.17.cloned.1.call-done), channel_id=1, replica_groups=mesh['dp'=8,'seq'=4] {'seq'}, dimensions={0}, use_global_device_ids=true | all-gather | bytes 327680 | tf_op jit(solution)/shard_map/all_gather | solution.py:93
  702.9 2.8 convert_element_type.288
  (161 shorter events, 33.8 us)
Async XLA Ops:
  7.2 311.7 %copy-start = (bf16[512,1024]{1,0:T(8,128)(2,1)S(1)}, bf16[512,1024]{1,0:T(8,128)(2,1)}, u32[]{:S(2)}) copy-start(bf16[512,1024]{1,0:T(8,128)(2,1)} %param.28) | copy-start | bytes 3145732
  7.2 3.2 copy-start.13
  7.2 87.8 %all-gather.12.cloned.1.call-start = ((), (), s32[]{:S(2)}) async-start(), calls=%async_computation.9 | async-start | bytes 5324800 | tf_op jit(solution)/shard_map/all_gather | solution.py:161
  10.2 2.0 copy-start.16
  10.2 2.3 copy-start.17
  10.2 2.5 copy-start.18
  10.2 2.7 copy-start.19
  10.2 2.9 copy-start.20
  10.2 3.1 copy-start.21
  10.3 3.2 copy-start.22
  10.3 111.6 %all-gather.14.cloned.1.call-start = ((), (), s32[]{:S(2)}) async-start(), calls=%async_computation.10 | async-start | bytes 1769472 | tf_op jit(solution)/shard_map/all_gather | solution.py:165
  11.5 192.4 %all-gather.16.cloned.1.call-start = ((), (), s32[]{:S(2)}) async-start(), calls=%async_computation.11 | async-start | bytes 2359296 | tf_op jit(solution)/shard_map/all_gather | solution.py:174
  12.2 241.6 %all-gather.24.cloned.1.call-start = ((), (), s32[]{:S(2)}) async-start(), calls=%async_computation.20 | async-start | bytes 4866048 | tf_op jit(solution)/shard_map/all_gather | solution.py:207
  98.0 1.4 copy-start.6
  199.4 4.4 copy-start.3
  206.5 1.0 copy-start.2
  208.5 102.6 %all-gather.22.cloned.1.call-start = ((), (), s32[]{:S(2)}) async-start(), calls=%async_computation.19 | async-start | bytes 9584640 | tf_op jit(solution)/shard_map/all_gather | solution.py:176
  211.4 6.6 copy-start.15
  213.7 21.4 %all-to-all-start.1 = ((bf16[128,8,512]{0,2,1:T(8,128)(2,1)}), bf16[128,8,512]{0,2,1:T(8,128)(2,1)}, u32[]{:S(2)}, u32[]{:S(2)}) async-start(bf16[128,8,512]{0,2,1:T(8,128)(2,1)} %bitcast.252), calls=%async_computation.1 | async-start | bytes 2097152 | tf_op jit(solution)/shard_map/all_to_all | solution.py:175
  218.0 324.6 %reduce-scatter.21.cloned.1.call-start = ((), (), s32[]{:S(2)}) async-start(), calls=%async_computation.17 | async-start | bytes 1310720 | tf_op jit(solution)/shard_map/reduce_scatter | solution.py:92
  318.9 241.4 %reduce-scatter.15.cloned.1.call-start = ((), (), s32[]{:S(2)}) async-start(), calls=%async_computation.13 | async-start | bytes 2359296 | tf_op jit(solution)/shard_map/reduce_scatter | solution.py:240
  318.9 6.2 copy-start.25
  318.9 6.2 copy-start.26
  325.1 5.9 copy-start.12
  329.6 1.4 copy-start.27
  335.4 95.3 %copy-start.24 = (u32[32]{0:T(128)S(1)}, u32[32]{0:T(128)}, u32[]{:S(2)}) copy-start(u32[32]{0:T(128)} %constant.110) | copy-start | bytes 388
  424.2 0.8 copy-start.10
  425.0 17.7 %copy-start.8 = (bf16[1,260,1024]{2,1,0:T(8,128)(2,1)S(1)}, bf16[1,260,1024]{2,1,0:T(8,128)(2,1)}, u32[]{:S(2)}) copy-start(bf16[1,260,1024]{2,1,0:T(8,128)(2,1)} %param.16) | copy-start | bytes 1597444
  425.0 6.9 collective-permute-start.1
  427.3 9.0 %collective-permute-start = (bf16[28,1024]{1,0:T(8,128)(2,1)S(1)}, bf16[28,1024]{1,0:T(8,128)(2,1)S(1)}, u32[]{:S(2)}, u32[]{:S(2)}) collective-permute-start(bf16[28,1024]{1,0:T(8,128)(2,1)S(1)} %slice.89), channel_id=1, source_target_pairs={{0,4},{4,8},{8,12},{12,16},{16,20},{20,24},{24,28},{1,5},{5,9},{9,... | collective-permute-start | bytes 172040
  442.7 4.1 copy-start.14
  445.9 1.0 copy-start.4
  464.0 19.4 %all-to-all-start.2 = ((bf16[4,2,33280]{2,1,0:T(2,128)(2,1)}), bf16[4,2,33280]{2,1,0:T(2,128)(2,1)S(1)}, u32[]{:S(2)}, u32[]{:S(2)}) async-start(bf16[4,2,33280]{2,1,0:T(2,128)(2,1)} %reshape.294), calls=%async_computation.2 | async-start | bytes 1064960 | tf_op jit(solution)/shard_map/all_to_all | solution.py:238
  483.4 35.8 %all-to-all-start.3 = ((bf16[8,128,512]{2,1,0:T(8,128)(2,1)}), bf16[8,128,512]{2,1,0:T(8,128)(2,1)}, u32[]{:S(2)}, u32[]{:S(2)}) async-start(bf16[8,128,512]{2,1,0:T(8,128)(2,1)} %bitcast.262), calls=%async_computation.6 | async-start | bytes 2097152 | tf_op jit(solution)/shard_map/all_to_all | solution.py:221
  487.9 118.4 %reduce-scatter.19.cloned.1.call-start = ((), (), s32[]{:S(2)}) async-start(), calls=%async_computation.15 | async-start | bytes 1310720 | tf_op jit(solution)/shard_map/reduce_scatter | solution.py:92
  521.6 130.4 %reduce-scatter.13.cloned.1.call-start = ((), (), s32[]{:S(2)}) async-start(), calls=%async_computation.12 | async-start | bytes 1769472 | tf_op jit(solution)/shard_map/reduce_scatter | solution.py:261
  527.2 9.6 %copy-start.11 = (bf16[1040,1,4,64]{0,3,2,1:T(8,128)(2,1)S(1)}, bf16[1040,1,4,64]{0,3,2,1:T(8,128)(2,1)}, u32[]{:S(2)}) copy-start(bf16[1040,1,4,64]{0,3,2,1:T(8,128)(2,1)} %fusion.30) | copy-start | bytes 1597444
  536.8 1.6 copy-start.7
  538.4 4.6 copy-start.23
  542.4 2.1 copy-start.9
  542.4 142.3 %all-gather.20.cloned.1.call-start = ((), (), s32[]{:S(2)}) async-start(), calls=%async_computation.18 | async-start | bytes 1310720 | tf_op jit(solution)/shard_map/all_gather | solution.py:93
  543.0 144.6 %reduce-scatter.17.cloned.1.call-start = ((), (), s32[]{:S(2)}) async-start(), calls=%async_computation.14 | async-start | bytes 327680 | tf_op jit(solution)/shard_map/reduce_scatter | solution.py:92
  560.3 142.6 %all-gather.18.cloned.1.call-start = ((), (), s32[]{:S(2)}) async-start(), calls=%async_computation.16 | async-start | bytes 1310720 | tf_op jit(solution)/shard_map/all_gather | solution.py:93
  600.8 50.0 %copy-start.5 = (f32[260,1024]{1,0:T(8,128)S(1)}, f32[260,1024]{1,0:T(8,128)}, u32[]{:S(2)}) copy-start(f32[260,1024]{1,0:T(8,128)} %copy-done.4) | copy-start | bytes 3194884
  601.0 4.6 collective-permute-start.2
  684.7 21.0 %copy-start.1 = (bf16[512,1024]{1,0:T(8,128)(2,1)S(1)}, bf16[512,1024]{1,0:T(8,128)(2,1)}, u32[]{:S(2)}) copy-start(bf16[512,1024]{1,0:T(8,128)(2,1)} %param.28) | copy-start | bytes 3145732
Sparse Core Ops, SparseCore 0:
  10.4 84.5 all-gather.11
  97.4 24.3 all-gather.13
  123.8 27.8 all-gather.15
  208.6 45.1 all-gather.23
  256.1 54.9 all-gather.21
  319.0 27.1 reduce-scatter.20
  449.6 41.6 reduce-scatter.14
  521.8 26.5 reduce-scatter.18
  552.6 37.1 reduce-scatter.12
  591.2 27.9 all-gather.19
  621.6 19.6 reduce-scatter.16
  642.8 39.3 all-gather.17

commit v2 on v1

v2 whole, which is shorter than its diff:
```python
import functools
import math

import jax
import jax.numpy as jnp
from jax import lax
from jax.experimental import pallas as pl
from jax.experimental.pallas import tpu as pltpu
from jax.sharding import PartitionSpec as P

HD = 64


EPSILON = 1e-05
ROOT_HALF = 0.7071067811865476
GAUSS_DENSITY = 0.3989422804014327
NEG_LARGE = -1e30


def norm_forward(values, gain_vec, shift_vec):
    mean_val = jnp.mean(values, axis=-1, keepdims=True)
    centred = values - mean_val
    inv_std = lax.rsqrt(jnp.mean(centred * centred, axis=-1, keepdims=True) + EPSILON)
    normed = centred * inv_std
    return (normed, inv_std, normed * gain_vec.astype(jnp.float32) + shift_vec.astype(jnp.float32))


def norm_backward(upstream, normed, inv_std, gain_vec):
    scaled = upstream * gain_vec.astype(jnp.float32)
    first_mean = jnp.mean(scaled, axis=-1, keepdims=True)
    second_mean = jnp.mean(scaled * normed, axis=-1, keepdims=True)
    return inv_std * (scaled - first_mean - normed * second_mean)


def gelu_value(preact):
    return 0.5 * preact * (1.0 + lax.erf(preact * ROOT_HALF))


def gelu_slope(preact):
    return (
        0.5 * (1.0 + lax.erf(preact * ROOT_HALF))
        + preact * jnp.exp(-0.5 * preact * preact) * GAUSS_DENSITY
    )


def against(left_mat, right_mat):
    return lax.dot_general(
        left_mat, right_mat, (((1,), (1,)), ((), ())), preferred_element_type=jnp.float32
    )


def outer_sum(left_mat, right_mat):
    return lax.dot_general(
        left_mat, right_mat, (((0,), (0,)), ((), ())), preferred_element_type=jnp.float32
    )


def forward_kernel(factor, chunk, live_ref, q_ref, k_ref, v_ref, out_ref, lse_ref):
    rows = q_ref.shape[0]
    live = live_ref[...] > 0.0
    values = v_ref[...].astype(jnp.float32).T.astype(jnp.bfloat16)
    for start in range(0, rows, chunk):
        parts = []
        for head in range(q_ref.shape[1] // HD):
            lanes = slice(head * HD, (head + 1) * HD)
            queries = q_ref[start : start + chunk, lanes] * jnp.bfloat16(factor)
            logits = jnp.where(live, against(k_ref[:, lanes], queries), NEG_LARGE)
            top = jnp.max(logits, axis=0, keepdims=True)
            powers = jnp.exp(logits - top)
            total = jnp.sum(powers, axis=0, keepdims=True)
            lse_ref[head : head + 1, start : start + chunk] = top + jnp.log(total)
            probs = (powers * (1.0 / total)).astype(jnp.bfloat16)
            parts.append(jnp.dot(values[lanes], probs, preferred_element_type=jnp.float32))
        merged = jnp.concatenate(parts, axis=0).T
        out_ref[start : start + chunk, :] = merged.astype(jnp.bfloat16)


def backward_kernel(
    factor,
    chunk,
    live_ref,
    q_ref,
    k_ref,
    v_ref,
    out_ref,
    lse_ref,
    grad_ref,
    dq_ref,
    dk_ref,
    dv_ref,
    dk_sum,
    dv_sum,
):
    rows = q_ref.shape[0]
    live = live_ref[...] > 0.0
    keys_t = k_ref[...].astype(jnp.float32).T.astype(jnp.bfloat16)
    for start in range(0, rows, chunk):
        span = slice(start, start + chunk)
        grads = grad_ref[span, :]
        dots = (grads.astype(jnp.float32) * out_ref[span, :].astype(jnp.float32)).T
        parts = []
        for head in range(q_ref.shape[1] // HD):
            lanes = slice(head * HD, (head + 1) * HD)
            queries = q_ref[span, lanes]
            grad = grads[:, lanes]
            delta = jnp.sum(dots[lanes], axis=0, keepdims=True) * factor
            logits = jnp.where(
                live, against(k_ref[:, lanes], queries * jnp.bfloat16(factor)), NEG_LARGE
            )
            probs = jnp.exp(logits - lse_ref[head : head + 1, span])
            d_probs = against(v_ref[:, lanes], grad * jnp.bfloat16(factor))
            d_logits = (probs * (d_probs - delta)).astype(jnp.bfloat16)
            dv_new = jnp.dot(
                probs.astype(jnp.bfloat16), grad, preferred_element_type=jnp.float32
            )
            dk_new = jnp.dot(d_logits, queries, preferred_element_type=jnp.float32)
            if start == 0:
                dv_sum[:, lanes] = dv_new
                dk_sum[:, lanes] = dk_new
            else:
                dv_sum[:, lanes] += dv_new
                dk_sum[:, lanes] += dk_new
            parts.append(jnp.dot(keys_t[lanes], d_logits, preferred_element_type=jnp.float32))
        dq_ref[span, :] = jnp.concatenate(parts, axis=0).T.astype(jnp.bfloat16)
    dk_ref[...] = dk_sum[...].astype(jnp.bfloat16)
    dv_ref[...] = dv_sum[...].astype(jnp.bfloat16)


def attention_specs(rows, pairs):
    live = pl.BlockSpec((None, rows, 1), lambda i, j: (i, 0, 0))
    part = [
        pl.BlockSpec((rows, 2 * HD), functools.partial(lambda c, i, j: (i, c * pairs + j), c))
        for c in range(3)
    ]
    lse = pl.BlockSpec((None, None, 2, rows), lambda i, j: (i, j, 0, 0))
    return live, part, lse


def chunk_of(rows):
    return 384 if rows % 384 == 0 else 128


def attention_forward(projected, live, images, factor):
    rows = projected.shape[0] // images
    pairs = projected.shape[1] // (6 * HD)
    live_spec, part, lse_spec = attention_specs(rows, pairs)
    work = images * pairs * 2 * rows * rows
    return pl.pallas_call(
        functools.partial(forward_kernel, factor, chunk_of(rows)),
        grid=(images, pairs),
        in_specs=[live_spec, *part],
        out_specs=[part[0], lse_spec],
        out_shape=[
            jax.ShapeDtypeStruct((images * rows, pairs * 2 * HD), jnp.bfloat16),
            jax.ShapeDtypeStruct((images, pairs, 2, rows), jnp.float32),
        ],
        compiler_params=pltpu.CompilerParams(vmem_limit_bytes=48 * 2**20),
        cost_estimate=pl.CostEstimate(
            flops=4 * work * HD, bytes_accessed=8 * projected.size // 3, transcendentals=work
        ),
        name="attention_forward",
    )(live, projected, projected, projected)


def attention_backward(projected, live, attended, lse, d_heads, images, factor):
    rows = projected.shape[0] // images
    pairs = projected.shape[1] // (6 * HD)
    live_spec, part, lse_spec = attention_specs(rows, pairs)
    work = images * pairs * 2 * rows * rows
    shape = jax.ShapeDtypeStruct((images * rows, pairs * 2 * HD), jnp.bfloat16)
    return pl.pallas_call(
        functools.partial(backward_kernel, factor, chunk_of(rows)),
        grid=(images, pairs),
        in_specs=[live_spec, *part, part[0], lse_spec, part[0]],
        out_specs=[part[0]] * 3,
        out_shape=[shape] * 3,
        scratch_shapes=[pltpu.VMEM((rows, 2 * HD), jnp.float32)] * 2,
        compiler_params=pltpu.CompilerParams(vmem_limit_bytes=48 * 2**20),
        cost_estimate=pl.CostEstimate(
            flops=10 * work * HD, bytes_accessed=16 * projected.size // 3, transcendentals=work
        ),
        name="attention_backward",
    )(live, projected, projected, projected, attended, lse, d_heads)


def shift(block, step):
    groups = lax.axis_size("seq")
    pairs = [(place, (place + step) % groups) for place in range(groups)]
    return lax.ppermute(block, "seq", pairs)


def turned(array, by):
    return lax.dynamic_slice_in_dim(jnp.concatenate([array, array]), by, array.shape[0])


def pad_rows(array, rows, axis=0):
    widths = [(0, 0)] * array.ndim
    widths[axis] = (0, rows - array.shape[axis])
    return jnp.pad(array, widths)


def extra_rows(vectors, owners, width):
    row = jnp.concatenate([vec.reshape(owners, 1, -1) for vec in vectors], axis=2)
    row = jnp.pad(row, ((0, 0), (0, 15), (0, width - row.shape[2])))
    return row.astype(jnp.bfloat16)


def shards(
    inputs,
    cotangent,
    valid_len,
    ln1_gain,
    ln1_bias,
    w_qkv,
    b_qv,
    w_out,
    b_out,
    ln2_gain,
    ln2_bias,
    w_up,
    b_up,
    w_down,
    b_down,
):
    images, shard_len, width = inputs.shape
    groups = lax.axis_size("seq")
    owners = lax.axis_size("dp")
    my_seq = lax.axis_index("seq")
    local_width = width // groups
    rows_owned = w_qkv.shape[0]
    hidden_local = w_down.shape[0]
    factor = 1.0 / math.sqrt(HD)
    bf16, f32 = jnp.bfloat16, jnp.float32

    step = math.lcm(16, 128 // math.gcd(groups, 128))
    padded = -(-shard_len // step) * step
    mlp_len = -(-shard_len // 16) * 16
    rows = images * padded
    seq_len = groups * padded

    inputs_pad = pad_rows(inputs, padded, 1)
    slots = [inputs_pad] + [shift(inputs_pad, k) for k in range(1, groups)]
    vectors = (ln1_gain, ln1_bias, b_out, ln2_gain, ln2_bias, b_down, b_qv)
    packed = lax.all_gather(jnp.concatenate(vectors), "dp", axis=0, tiled=False)
    pieces = []
    offset = 0
    for vec in vectors:
        pieces.append(packed[:, offset : offset + vec.shape[0]].reshape(-1))
        offset += vec.shape[0]
    gain_one, bias_one, out_bias, gain_two, bias_two, down_bias, qv_bias = pieces
    qkv_slice = lax.dynamic_slice_in_dim(
        w_qkv.reshape(rows_owned, 3, groups, local_width), my_seq, 1, axis=2
    ).reshape(rows_owned, 3 * local_width)
    qkv_cols = lax.all_gather(qkv_slice, "dp", axis=0, tiled=True)
    out_full = turned(lax.all_gather(w_out, "dp", axis=0, tiled=True), my_seq * local_width)
    up_cols = lax.all_to_all(w_up, "dp", split_axis=1, concat_axis=0, tiled=True)
    cot_mine = pad_rows(cotangent, mlp_len, 1).reshape(images * mlp_len, width)
    cot_all = lax.all_gather(cot_mine, "dp", axis=0, tiled=True)

    place = jnp.arange(seq_len)
    source = lax.rem(my_seq - place // padded + groups, groups)
    within = place % padded
    token_id = jnp.where(within < shard_len, source * shard_len + within, groups * shard_len)
    live = (token_id[None, :] < valid_len[:, None]).astype(f32)[:, :, None]

    rows_all = jnp.concatenate(slots, axis=1).reshape(images * seq_len, width)
    normed_all, _, pre_all = norm_forward(rows_all.astype(f32), gain_one, bias_one)
    hidden_one = pre_all.astype(bf16)
    qkv_bias = jnp.concatenate(
        [qv_bias[:width], jnp.zeros((width,), bf16), qv_bias[width:]]
    ).reshape(3, groups, local_width)
    qkv_bias = lax.dynamic_slice_in_dim(qkv_bias, my_seq, 1, axis=1).reshape(-1).astype(f32)
    projected = (
        jnp.dot(hidden_one, qkv_cols, preferred_element_type=f32) + qkv_bias
    ).astype(bf16)
    attended, lse = attention_forward(projected, live, images, factor)
    by_slot = attended.reshape(images, groups, padded, local_width)
    heads = [by_slot[:, 0]] + [shift(by_slot[:, k], -k) for k in range(1, groups)]
    merged_rows = jnp.concatenate(heads, axis=2).reshape(rows, width)
    token_rows = inputs_pad.reshape(rows, width).astype(f32)
    residual = (
        token_rows
        + jnp.dot(merged_rows, out_full, preferred_element_type=f32)
        + out_bias.astype(f32)
    )
    normed_two, inv_two, pre_two = norm_forward(residual, gain_two, bias_two)

    def to_mlp(array):
        return array.reshape(images, padded, width)[:, :mlp_len].reshape(-1, width)

    def from_mlp(array):
        whole = array.astype(f32).reshape(images, mlp_len, width)
        return pad_rows(whole, padded, 1).reshape(rows, width)

    def scatter(array):
        blocks = array.reshape(owners, images * mlp_len, width)
        return lax.psum_scatter(blocks, "dp", scatter_dimension=0, tiled=False)

    hidden_two = lax.all_gather(to_mlp(pre_two.astype(bf16)), "dp", axis=0, tiled=True)
    d_act = against(cot_all, w_down)
    preact = jnp.dot(hidden_two, up_cols, preferred_element_type=f32) + b_up.astype(f32)
    activated = gelu_value(preact).astype(bf16)
    d_preact = d_act * gelu_slope(preact)
    grad_hidden = d_preact.astype(bf16)
    d_second = from_mlp(scatter(against(grad_hidden, up_cols).astype(bf16)))
    mlp_part = jnp.dot(activated, w_down, preferred_element_type=f32).astype(bf16)
    mlp_sum = from_mlp(scatter(mlp_part))
    outputs = (residual + mlp_sum + down_bias.astype(f32)).astype(bf16)
    outputs = outputs.reshape(images, padded, width)[:, :shard_len]
    bias_up = jnp.sum(d_preact, axis=0)
    bias_row = jnp.pad(bias_up[None, :], ((0, 15), (0, width - hidden_local)))
    grad_down = jnp.concatenate([outer_sum(activated, cot_all), bias_row]).astype(bf16)
    grad_up = lax.all_to_all(
        outer_sum(hidden_two, grad_hidden).astype(bf16),
        "dp",
        split_axis=0,
        concat_axis=1,
        tiled=True,
    )
    grad_down, grad_up = lax.psum((grad_down, grad_up), "seq")
    own_up = grad_down[hidden_local, :hidden_local].astype(f32)
    grad_down = grad_down[:hidden_local].astype(f32)
    grad_up = grad_up.astype(f32)

    cot_rows = from_mlp(cot_mine)
    bias_down = jnp.sum(cot_rows, axis=0)
    second_gain = jnp.sum(d_second * normed_two, axis=0)
    second_shift = jnp.sum(d_second, axis=0)
    d_residual = cot_rows + norm_backward(d_second, normed_two, inv_two, gain_two)
    res_bf = d_residual.astype(bf16)
    d_merged = against(res_bf, out_full).astype(bf16).reshape(images, padded, width)
    grads = [
        d_merged[:, :, k * local_width : (k + 1) * local_width] for k in range(groups)
    ]
    grads = [grads[0]] + [shift(grads[k], k) for k in range(1, groups)]
    d_heads = jnp.concatenate(grads, axis=1).reshape(images * seq_len, local_width)
    bias_out = jnp.sum(d_residual, axis=0)
    grad_out = turned(
        outer_sum(merged_rows, res_bf).astype(bf16), (groups - my_seq) * local_width
    ).reshape(owners, rows_owned, width)
    small = extra_rows((second_gain, second_shift, bias_out, bias_down), owners, width)
    grad_out = lax.psum_scatter(
        jnp.concatenate([grad_out, small], axis=1), "dp", scatter_dimension=0, tiled=False
    )
    grad_out = lax.psum(grad_out, "seq").astype(f32)
    small = grad_out[rows_owned, : 4 * rows_owned].reshape(4, rows_owned)
    own_second_gain, own_second_shift, own_out, own_down = small
    grad_out = grad_out[:rows_owned]

    d_proj = jnp.concatenate(
        attention_backward(projected, live, attended, lse, d_heads, images, factor), axis=1
    )
    d_part = against(d_proj, qkv_cols)
    first_gain = jnp.sum(d_part * normed_all, axis=0)
    first_shift = jnp.sum(d_part, axis=0)
    by_slot = d_part.astype(bf16).reshape(images, groups, padded, width)
    d_first = by_slot[:, 0].astype(f32)
    for k in range(1, groups):
        d_first += shift(by_slot[:, k], -k).astype(f32)
    d_first = d_first.reshape(rows, width)
    summed = jnp.sum(d_proj.astype(f32), axis=0).reshape(3, 1, local_width)
    bias_qv = lax.dynamic_update_slice(
        jnp.zeros((2, groups, local_width), f32),
        jnp.concatenate([summed[:1], summed[2:]], axis=0),
        (0, my_seq, 0),
    ).reshape(-1)
    small = extra_rows((first_gain, first_shift, bias_qv), owners, 3 * local_width)
    grad_qkv = outer_sum(hidden_one, d_proj).astype(bf16)
    grad_qkv = jnp.concatenate(
        [grad_qkv.reshape(owners, rows_owned, 3 * local_width), small], axis=1
    )
    grad_qkv = lax.psum_scatter(grad_qkv, "dp", scatter_dimension=0, tiled=False)
    grad_qkv = lax.all_gather(grad_qkv, "seq", axis=0, tiled=False).astype(f32)
    small = jnp.sum(grad_qkv[:, rows_owned], axis=0)
    own_gain = small[:rows_owned]
    own_shift = small[rows_owned : 2 * rows_owned]
    own_qv = small[2 * rows_owned : 4 * rows_owned]
    grad_qkv = (
        grad_qkv[:, :rows_owned]
        .reshape(groups, rows_owned, 3, local_width)
        .transpose(1, 2, 0, 3)
        .reshape(rows_owned, 3 * width)
    )
    normed_one, inv_one, _ = norm_forward(token_rows, gain_one, bias_one)
    d_inputs = (d_residual + norm_backward(d_first, normed_one, inv_one, gain_one)).astype(bf16)
    d_inputs = d_inputs.reshape(images, padded, width)[:, :shard_len]
    return (
        outputs,
        d_inputs,
        own_gain,
        own_shift,
        grad_qkv,
        own_qv,
        grad_out,
        own_out,
        own_second_gain,
        own_second_shift,
        grad_up,
        own_up,
        grad_down,
        own_down,
    )


def solution(mesh):
    placed = (
        P("dp", "seq", None),
        P("dp", "seq", None),
        P("dp"),
        P("dp"),
        P("dp"),
        P("dp", None),
        P("dp"),
        P("dp", None),
        P("dp"),
        P("dp"),
        P("dp"),
        P("dp", None),
        P("dp"),
        P("dp", None),
        P("dp"),
    )
    return jax.shard_map(
        shards,
        mesh=mesh,
        in_specs=placed,
        out_specs=(
            P("dp", "seq", None),
            P("dp", "seq", None),
            P("dp"),
            P("dp"),
            P("dp", None),
            P("dp"),
            P("dp", None),
            P("dp"),
            P("dp"),
            P("dp"),
            P("dp", None),
            P("dp"),
            P("dp", None),
            P("dp"),
        ),
        check_vma=False,
    )
```

time: 720 us -> 573 us (0.80)
  blocking collectives: 257 us -> 28.9 us
  waiting for transfers between devices: 181 us -> 349 us
  local copies, waits for them, and re-layouts: 81 us -> 26.8 us
  matrix products: 112 us -> 58.7 us
  Pallas kernels: 0 us -> 27.3 us
  other arithmetic: 44 us -> 27.5 us
  starting transfers between devices: 21 us -> 30.1 us
    unnamed x2 -> x0, blocking collectives: 129 us -> none
    ppermute x0 -> x12, waiting for transfers between devices: none -> 129 us  [shift(): return lax.ppermute(block, 'seq', pairs)]
    reduce_scatter x5 -> x4, waiting for transfers between devices: 0.04 us -> 100 us  [the longest x2 100 us: scatter(): return lax.psum_scatter(blocks, 'dp', scatter_dimension=0, tiled=False)]
    all_gather x6 -> x3, waiting for transfers between devices: 131 us -> 50.8 us  [the longest x1 31.2 us: shards(): cot_all = lax.all_gather(cot_mine, 'dp', axis=0, tiled=True)]
    dot_general x6 -> x0, matrix products: 52.5 us -> none  [the longest x1 11 us: attend_backward(): jnp.einsum('qhe,khe->hqk', d_output, values_in, preferred_element_type=jn...]
    psum x2 -> x0, blocking collectives: 52.5 us -> none  [the longest x1 41.9 us: owned(): sums = lax.psum(jnp.concatenate(parts), ('dp', 'seq'))]
    psum x0 -> x1, waiting for transfers between devices: none -> 38.4 us  [shards(): grad_out = lax.psum(grad_out, 'seq').astype(f32)]
    unnamed x84 -> x91, local copies, waits for them, and re-layouts: 43.7 us -> 12.4 us
  transfers between devices with their start and end apart: 18 -> 23, of which waited for: 7 -> 15; matrix products, arithmetic and copies ran while one was open for 48% -> 13% of each run, Pallas kernels for 0% -> 5%
where the time goes in v2:
time: 573 us; the launch traced here: 563 us
  waiting for transfers between devices  349 us (61%)
  matrix products  58.7 us (10%)
  starting transfers between devices  30.1 us (5%)
  blocking collectives  28.9 us (5%)
  other arithmetic  27.5 us (5%)
  Pallas kernels  27.3 us (5%)
  local copies, waits for them, and re-layouts  26.8 us (5%)
  between operations  15.4 us (3%)
    ppermute x12, waiting for transfers between devices, shift(): return lax.ppermute(block, 'seq', pairs)  129 us
    reduce_scatter x2, waiting for transfers between devices, scatter(): return lax.psum_scatter(blocks, 'dp', scatter_dimension=0, tiled=False)  100 us
    psum x1, waiting for transfers between devices, shards(): grad_out = lax.psum(grad_out, 'seq').astype(f32)  38.4 us
    all_gather x1, waiting for transfers between devices, shards(): cot_all = lax.all_gather(cot_mine, 'dp', axis=0, tiled=True)  31.2 us
    ppermute x12, starting transfers between devices, shift(): return lax.ppermute(block, 'seq', pairs)  21.3 us
    all_to_all x1, waiting for transfers between devices, shards(): lax.all_to_all(w_up, 'dp', split_axis=1, concat_axis=0, tiled=True)  21.3 us
    dot_general x4, matrix products, against(): lax.dot_general(left_mat, right_mat, (((1,), (1,)), ((), ())), preferred_...  20.4 us
    all_gather x1, blocking collectives, shards(): grad_qkv = lax.all_gather(grad_qkv, 'seq', axis=0, tiled=False).astype(f32)  20 us
  transfers between devices with their start and end apart: 23, of which 15 were waited for; matrix products, arithmetic and copies ran while one was open for 13% of the time, Pallas kernels for 5%

profile of v2, /device:TPU:0, one launch (start us, length us, event | category | flops | bytes accessed | tf_op | source)
XLA Modules:
  0.0 563.4 jit_solution(842288338088864705)
XLA Ops:
  7.3 1.6 copy.44
  10.5 5.1 collective-permute-start.2
  15.6 1.0 collective-permute-start
  18.8 8.9 %all-gather = bf16[8192]{0:T(1024)(128)(2,1)S(1)} all-gather(bf16[1024]{0:T(1024)(128)(2,1)S(1)} %dynamic-update-slice.9), channel_id=2, replica_groups=mesh['dp'=8,'seq'=4] {'dp'}, dimensions={0}, use_global_device_ids=true | all-gather | bytes 18432 | tf_op jit(solution)/shard_map/all_gather | solution.py:244
  28.4 1.1 collective-permute-done.2
  29.4 36.6 %collective-permute-done.1 = bf16[1,288,1024]{2,1,0:T(8,128)(2,1)S(1)} collective-permute-done((bf16[1,288,1024]{2,1,0:T(8,128)(2,1)S(1)}, bf16[1,288,1024]{2,1,0:T(8,128)(2,1)S(1)}, u32[]{:S(2)}, u32[]{:S(2)}) %collective-permute-start.1) | collective-permute-done | bytes 589856 | tf_op jit(solution)/shard_map/ppermute | solution.py:189
  66.0 1.7 convert_reduce_fusion
  67.7 2.1 fusion.8
  69.8 4.0 fusion.21.q_ref.k_ref.v_ref
  73.8 11.2 %attention_forward.1 = (bf16[1152,256]{1,0:T(8,128)(2,1)S(1)}, f32[1,2,2,1152]{3,2,1,0:T(2,128)S(1)}) custom-call(f32[1,1152,1]{2,1,0:T(8,128)S(1)} %fusion.80.live_ref, bf16[1152,768]{1,0:T(8,128)(2,1)S(1)} %fusion.21.q_ref.k_ref.v_ref, bf16[1152,768]{1,0:T(8,128)(2,1)S(1)} %fusion.21.q_ref.k_ref.v_ref, bf16[1152,768]{1,0:T(8,128)(2,1)S(1)} %fusion.21.q_ref.k_ref.v_ref), custom_call_target="tpu_custom_call" | custom-call | flops 1358954496 | bytes 2359296 | tf_op jit(solution)/shard_map/attention_forward/pallas_call | solution.py:148
  86.7 2.1 collective-permute-start.4
  88.8 2.8 collective-permute-start.3
  91.7 2.9 collective-permute-done.5
  94.6 4.5 collective-permute-done.4
  99.8 3.4 fusion.104
  104.8 1.9 pad.42
  106.7 2.3 copy.45
  109.0 4.2 all-to-all-start
  113.3 21.3 %all-to-all-done = bf16[128,8,512]{0,2,1:T(8,128)(2,1)} async-done(((bf16[128,8,512]{0,2,1:T(8,128)(2,1)}), bf16[128,8,512]{0,2,1:T(8,128)(2,1)}, u32[]{:S(2)}, u32[]{:S(2)}) %all-to-all-start) | async-done | bytes 1048608 | tf_op jit(solution)/shard_map/all_to_all | solution.py:256
  134.6 2.3 copy.46
  136.8 19.7 %all-gather.12.cloned.1.call-done = bf16[1,2176,1024]{2,1,0:T(8,128)(2,1)} async-done(((bf16[1,272,1024]{2,1,0:T(8,128)(2,1)}), bf16[1,2176,1024]{2,1,0:T(8,128)(2,1)}) %all-gather.12.cloned.1.call-update) | async-done | bytes 4456464 | tf_op jit(solution)/shard_map/all_gather | solution.py:299
  156.5 8.4 %multiply_convert_fusion = (bf16[2176,512]{1,0:T(8,128)(2,1)}, f32[2176,512]{1,0:T(8,128)}) fusion(f32[512]{0:T(512)S(1)} %convert_element_type.231, bf16[1024,512]{1,0:T(8,128)(2,1)} %bitcast.232, bf16[1,2176,1024]{2,1,0:T(8,128)(2,1)} %all-gather.12.cloned.1.call-done), kind=kOutput, calls=%fused_computation.28 | convolution fusion | flops 2288386048 | bytes 12191744 | tf_op jit(solution)/shard_map/dot_general | solution.py:301
  164.9 31.2 %all-gather.14.cloned.1.call-done = bf16[1,2176,1024]{2,1,0:T(8,128)(2,1)} async-done(((bf16[1,272,1024]{2,1,0:T(8,128)(2,1)}), bf16[1,2176,1024]{2,1,0:T(8,128)(2,1)}) %all-gather.14.cloned.1.call-update) | async-done | bytes 4456464 | tf_op jit(solution)/shard_map/all_gather | solution.py:258
  196.1 6.9 %fusion.105 = (bf16[512]{0:T(512)(128)(2,1)S(1)}, bf16[2176,512]{1,0:T(8,128)(2,1)S(1)}) fusion(f32[2176,512]{1,0:T(8,128)} %get-tuple-element.97, bf16[512,1024]{1,0:T(8,128)(2,1)S(1)} %copy-done, bf16[1,2176,1024]{2,1,0:T(8,128)(2,1)} %all-gather.14.cloned.1.call-done), kind=kOutput, calls=%fused_computation.184 | convolution fusion | flops 2293956096 | bytes 12190720 | tf_op jit(solution)/shard_map/dot_general | solution.py:47
  203.0 4.7 convolution_convert_fusion
  207.8 6.2 %convolution_convert_fusion.1 = bf16[2176,1024]{1,0:T(8,128)(2,1)} fusion(bf16[2176,512]{1,0:T(8,128)(2,1)} %get-tuple-element.96, bf16[512,1024]{1,0:T(8,128)(2,1)S(1)} %copy-done), kind=kOutput, calls=%fused_computation.4 | convolution fusion | flops 2283929600 | bytes 7733248 | tf_op jit(solution)/shard_map/dot_general | solution.py:306
  215.1 45.5 %reduce-scatter.7.cloned.1.call-done = bf16[1,272,1024]{2,1,0:T(8,128)(2,1)} async-done(((bf16[8,272,1024]{2,1,0:T(8,128)(2,1)}), bf16[1,272,1024]{2,1,0:T(8,128)(2,1)}) %reduce-scatter.7.cloned.1.call-update) | async-done | bytes 557072 | tf_op jit(solution)/shard_map/reduce_scatter | solution.py:297
  260.6 1.6 fusion.54
  262.2 54.8 %reduce-scatter.5.cloned.1.call-done = bf16[1,272,1024]{2,1,0:T(8,128)(2,1)} async-done(((bf16[8,272,1024]{2,1,0:T(8,128)(2,1)}), bf16[1,272,1024]{2,1,0:T(8,128)(2,1)}) %reduce-scatter.5.cloned.1.call-update) | async-done | bytes 557072 | tf_op jit(solution)/shard_map/reduce_scatter | solution.py:297
  317.0 2.8 fusion.98
  319.9 2.1 fusion.43
  322.2 3.4 collective-permute-start.8
  325.6 1.1 collective-permute-start.6
  326.7 1.3 convolution_convert_fusion.2
  328.0 2.8 fusion.24
  330.8 1.8 fusion.22
  333.1 5.1 collective-permute-done.7
  338.3 1.6 copy-done.3
  339.9 16.0 %attention_backward.1 = (bf16[1152,256]{1,0:T(8,128)(2,1)S(1)}, bf16[1152,256]{1,0:T(8,128)(2,1)S(1)}, bf16[1152,256]{1,0:T(8,128)(2,1)S(1)}) custom-call(f32[1,1152,1]{2,1,0:T(8,128)S(1)} %fusion.80.live_ref, bf16[1152,768]{1,0:T(8,128)(2,1)S(1)} %copy-done.3, bf16[1152,768]{1,0:T(8,128)(2,1)S(1)} %copy-done.3, bf16[1152,768]{1,0:T(8,128)(2,1)S(1)} %copy-done.3, ...), custom_call_target="tpu_custom_call" | custom-call | flops 3397386240 | bytes 4718592 | tf_op jit(solution)/shard_map/attention_backward/pallas_call | solution.py:171
  357.2 6.7 %fusion.7 = (bf16[1024]{0:T(1024)(128)(2,1)S(1)}, bf16[1024]{0:T(1024)(128)(2,1)S(1)}, bf16[1152,1024]{1,0:T(8,128)(2,1)}) fusion(f32[1152]{0:T(1024)S(1)} %add_rsqrt_fusion, f32[1152]{0:T(1024)S(1)} %broadcast_multiply_fusion, bf16[1,288,1024]{2,1,0:T(8,128)(2,1)S(1)} %copy-done.14, bf16[1,288,1024]{2,1,0:T(8,128)(2,1)} %copy-done.15, ...), kind=kOutput, calls=%fused_computation.14 | convolution fusion | flops 1828452352 | bytes 8074240 | tf_op jit(solution)/shard_map/dot_general | solution.py:47
  363.9 3.7 convolution_convert_fusion.3
  367.6 1.3 fusion.26
  368.9 1.0 copy-done.38
  369.9 5.9 %fusion.27 = bf16[1024,512]{1,0:T(8,128)(2,1)} fusion(bf16[1,2176,1024]{2,1,0:T(8,128)(2,1)} %all-gather.12.cloned.1.call-done, bf16[2176,512]{1,0:T(8,128)(2,1)S(1)} %copy-done.38), kind=kOutput, calls=%fused_computation.49 | convolution fusion | flops 2282225664 | bytes 7733248 | tf_op jit(solution)/shard_map/dot_general | solution.py:53
  375.8 3.6 all-to-all-start.1
  379.4 5.6 fusion.30
  385.0 1.1 fusion.63
  386.0 8.7 %all-to-all-done.1 = bf16[8,128,512]{2,1,0:T(8,128)(2,1)S(1)} async-done(((bf16[8,128,512]{2,1,0:T(8,128)(2,1)}), bf16[8,128,512]{2,1,0:T(8,128)(2,1)S(1)}, u32[]{:S(2)}, u32[]{:S(2)}) %all-to-all-start.1) | async-done | bytes 1048608 | tf_op jit(solution)/shard_map/all_to_all | solution.py:313
  394.7 1.1 copy.55
  396.9 1.3 collective-permute-start.9
  399.0 2.8 collective-permute-start.10
  403.1 17.4 %collective-permute-done.9 = bf16[1,288,1024]{2,1,0:T(8,128)(2,1)S(1)} collective-permute-done((bf16[1,288,1024]{2,1,0:T(8,128)(2,1)S(1)}, bf16[1,288,1024]{2,1,0:T(8,128)(2,1)S(1)}, u32[]{:S(2)}, u32[]{:S(2)}) %collective-permute-start.9) | collective-permute-done | bytes 589856 | tf_op jit(solution)/shard_map/ppermute | solution.py:189
  420.5 7.7 %collective-permute-done.11 = bf16[1,288,1024]{2,1,0:T(8,128)(2,1)S(1)} collective-permute-done((bf16[1,288,1024]{2,1,0:T(8,128)(2,1)S(1)}, bf16[1,288,1024]{2,1,0:T(8,128)(2,1)S(1)}, u32[]{:S(2)}, u32[]{:S(2)}) %collective-permute-start.11) | collective-permute-done | bytes 589856 | tf_op jit(solution)/shard_map/ppermute | solution.py:189
  428.2 53.2 %collective-permute-done.10 = bf16[1,288,1024]{2,1,0:T(8,128)(2,1)S(1)} collective-permute-done((bf16[1,288,1024]{2,1,0:T(8,128)(2,1)S(1)}, bf16[1,288,1024]{2,1,0:T(8,128)(2,1)S(1)}, u32[]{:S(2)}, u32[]{:S(2)}) %collective-permute-start.10) | collective-permute-done | bytes 589856 | tf_op jit(solution)/shard_map/ppermute | solution.py:189
  483.3 20.0 %all_gather.27 = bf16[4,144,768]{2,1,0:T(8,128)(2,1)S(1)} all-gather(bf16[1,144,768]{2,1,0:T(8,128)(2,1)} %reduce-scatter.9.cloned.1.call-done), channel_id=1, replica_groups=mesh['dp'=8,'seq'=4] {'seq'}, dimensions={0}, use_global_device_ids=true | all-gather | bytes 1105920 | tf_op jit(solution)/shard_map/all_gather | solution.py:373
  504.0 1.9 convert_element_type.250
  506.1 1.6 copy.52
  507.7 1.6 slice_reduce_fusion
  510.4 38.4 %all-reduce.11.cloned.1.call-done = (bf16[144,1024]{1,0:T(8,128)(2,1)}, bf16[128,4096]{1,0:T(8,128)(2,1)}, bf16[528,1024]{1,0:T(8,128)(2,1)}) async-done(((bf16[144,1024]{1,0:T(8,128)(2,1)}, bf16[128,4096]{1,0:T(8,128)(2,1)}, bf16[528,1024]{1,0:T(8,128)(2,1)}), (bf16[144,1024]{1,0:T(8,128)(2,1)}, bf16[128,4096]{1,0:T(8,128)(2,1)}, bf16[528,1024]{1,0:T(8,128)(2,1)})) %all-reduce.11.cloned.1.call-update) | async-done | bytes 2424848 | tf_op jit(solution)/shard_map/psum | solution.py:345
  548.8 1.9 slice.179
  550.6 1.1 convert_element_type.252
  551.7 1.3 slice_convert_fusion.1
  553.0 1.6 slice_convert_fusion
  555.1 1.5 convert_element_type.254
  (168 shorter events, 18.4 us)
Async XLA Ops:
  7.2 188.9 %copy-start = (bf16[512,1024]{1,0:T(8,128)(2,1)S(1)}, bf16[512,1024]{1,0:T(8,128)(2,1)}, u32[]{:S(2)}) copy-start(bf16[512,1024]{1,0:T(8,128)(2,1)} %param.28) | copy-start | bytes 3145732
  7.2 3.3 copy-start.4
  7.2 10.1 %copy-start.23 = (bf16[128]{0:T(256)(128)(2,1)S(1)}, bf16[128]{0:T(256)(128)(2,1)}, u32[]{:S(2)}) copy-start(bf16[128]{0:T(256)(128)(2,1)} %param.18) | copy-start | bytes 772
  7.2 10.3 %copy-start.24 = (bf16[128]{0:T(256)(128)(2,1)S(1)}, bf16[128]{0:T(256)(128)(2,1)}, u32[]{:S(2)}) copy-start(bf16[128]{0:T(256)(128)(2,1)} %param.19) | copy-start | bytes 772
  7.2 10.5 %copy-start.25 = (bf16[128]{0:T(256)(128)(2,1)S(1)}, bf16[128]{0:T(256)(128)(2,1)}, u32[]{:S(2)}) copy-start(bf16[128]{0:T(256)(128)(2,1)} %param.23) | copy-start | bytes 772
  7.2 10.7 %copy-start.26 = (bf16[128]{0:T(256)(128)(2,1)S(1)}, bf16[128]{0:T(256)(128)(2,1)}, u32[]{:S(2)}) copy-start(bf16[128]{0:T(256)(128)(2,1)} %param.24) | copy-start | bytes 772
  7.3 10.9 %copy-start.27 = (bf16[128]{0:T(256)(128)(2,1)S(1)}, bf16[128]{0:T(256)(128)(2,1)}, u32[]{:S(2)}) copy-start(bf16[128]{0:T(256)(128)(2,1)} %param.25) | copy-start | bytes 772
  7.3 11.1 %copy-start.28 = (bf16[128]{0:T(256)(128)(2,1)S(1)}, bf16[128]{0:T(256)(128)(2,1)}, u32[]{:S(2)}) copy-start(bf16[128]{0:T(256)(128)(2,1)} %param.29) | copy-start | bytes 772
  7.3 11.3 %copy-start.29 = (bf16[256]{0:T(256)(128)(2,1)S(1)}, bf16[256]{0:T(256)(128)(2,1)}, u32[]{:S(2)}) copy-start(bf16[256]{0:T(256)(128)(2,1)} %param.21) | copy-start | bytes 1540
  7.3 62.5 %all-gather.8.cloned.1.call-start = ((), (), s32[]{:S(2)}) async-start(), calls=%async_computation.6 | async-start | bytes 1769472 | tf_op jit(solution)/shard_map/all_gather | solution.py:254
  9.7 89.5 %all-gather.10.cloned.1.call-start = ((), (), s32[]{:S(2)}) async-start(), calls=%async_computation.7 | async-start | bytes 2359296 | tf_op jit(solution)/shard_map/all_gather | solution.py:255
  10.4 146.1 %all-gather.12.cloned.1.call-start = ((), (), s32[]{:S(2)}) async-start(), calls=%async_computation.12 | async-start | bytes 5013504 | tf_op jit(solution)/shard_map/all_gather | solution.py:299
  10.5 59.3 %copy-start.7 = (bf16[1,288,1024]{2,1,0:T(8,128)(2,1)}, bf16[1,288,1024]{2,1,0:T(8,128)(2,1)S(1)}, u32[]{:S(2)}) copy-start(bf16[1,288,1024]{2,1,0:T(8,128)(2,1)S(1)} %pad.40) | copy-start | bytes 1769476
  10.5 18.9 %collective-permute-start.2 = (bf16[1,288,1024]{2,1,0:T(8,128)(2,1)S(1)}, bf16[1,288,1024]{2,1,0:T(8,128)(2,1)S(1)}, u32[]{:S(2)}, u32[]{:S(2)}) collective-permute-start(bf16[1,288,1024]{2,1,0:T(8,128)(2,1)S(1)} %pad.40), channel_id=1, source_target_pairs={{0,3},{1,0},{2,1},{3,2},{4,7},{5,4},{6,5},{7,6},{8,11},{9,8},{10,9... | collective-permute-start | bytes 1769480 | tf_op jit(solution)/shard_map/ppermute | solution.py:189
  15.6 50.4 %collective-permute-start.1 = (bf16[1,288,1024]{2,1,0:T(8,128)(2,1)S(1)}, bf16[1,288,1024]{2,1,0:T(8,128)(2,1)S(1)}, u32[]{:S(2)}, u32[]{:S(2)}) collective-permute-start(bf16[1,288,1024]{2,1,0:T(8,128)(2,1)S(1)} %pad.40), channel_id=1, source_target_pairs={{0,2},{1,3},{2,0},{3,1},{4,6},{5,7},{6,4},{7,5},{8,10},{9,11},{10,... | collective-permute-start | bytes 1769480 | tf_op jit(solution)/shard_map/ppermute | solution.py:189
  15.6 50.4 %collective-permute-start = (bf16[1,288,1024]{2,1,0:T(8,128)(2,1)S(1)}, bf16[1,288,1024]{2,1,0:T(8,128)(2,1)}, u32[]{:S(2)}, u32[]{:S(2)}) collective-permute-start(bf16[1,288,1024]{2,1,0:T(8,128)(2,1)S(1)} %pad.40), channel_id=1, source_target_pairs={{0,1},{1,2},{2,3},{3,0},{4,5},{5,6},{6,7},{7,4},{8,9},{9,10},{10,1... | collective-permute-start | bytes 1769480 | tf_op jit(solution)/shard_map/ppermute | solution.py:189
  29.4 40.4 %copy-start.13 = (bf16[1,288,1024]{2,1,0:T(8,128)(2,1)}, bf16[1,288,1024]{2,1,0:T(8,128)(2,1)S(1)}, u32[]{:S(2)}) copy-start(bf16[1,288,1024]{2,1,0:T(8,128)(2,1)S(1)} %collective-permute-done.2) | copy-start | bytes 1769476
  66.0 3.8 copy-start.15
  73.8 11.3 %copy-start.2 = (bf16[1152,768]{1,0:T(8,128)(2,1)}, bf16[1152,768]{1,0:T(8,128)(2,1)S(1)}, u32[]{:S(2)}) copy-start(bf16[1152,768]{1,0:T(8,128)(2,1)S(1)} %fusion.21.q_ref.k_ref.v_ref) | copy-start | bytes 5308420
  85.8 8.8 %collective-permute-start.5 = (bf16[1,288,256]{2,1,0:T(8,128)(2,1)S(1)}, bf16[1,288,256]{2,1,0:T(8,128)(2,1)S(1)}, u32[]{:S(2)}, u32[]{:S(2)}) collective-permute-start(bf16[1,288,256]{2,1,0:T(8,128)(2,1)S(1)} %get-tuple-element.79), channel_id=1, source_target_pairs={{0,1},{1,2},{2,3},{3,0},{4,5},{5,6},{6,7},{7,4},{8,9},{9,10},{10,1... | collective-permute-start | bytes 442376 | tf_op jit(solution)/shard_map/ppermute | solution.py:189
  86.7 12.4 %collective-permute-start.4 = (bf16[1,288,256]{2,1,0:T(8,128)(2,1)S(1)}, bf16[1,288,256]{2,1,0:T(8,128)(2,1)S(1)}, u32[]{:S(2)}, u32[]{:S(2)}) collective-permute-start(bf16[1,288,256]{2,1,0:T(8,128)(2,1)S(1)} %get-tuple-element.80), channel_id=1, source_target_pairs={{0,2},{1,3},{2,0},{3,1},{4,6},{5,7},{6,4},{7,5},{8,10},{9,11},{10,... | collective-permute-start | bytes 442376 | tf_op jit(solution)/shard_map/ppermute | solution.py:189
  88.8 10.3 %collective-permute-start.3 = (bf16[1,288,256]{2,1,0:T(8,128)(2,1)S(1)}, bf16[1,288,256]{2,1,0:T(8,128)(2,1)S(1)}, u32[]{:S(2)}, u32[]{:S(2)}) collective-permute-start(bf16[1,288,256]{2,1,0:T(8,128)(2,1)S(1)} %get-tuple-element.81), channel_id=1, source_target_pairs={{0,3},{1,0},{2,1},{3,2},{4,7},{5,4},{6,5},{7,6},{8,11},{9,8},{10,9... | collective-permute-start | bytes 442376 | tf_op jit(solution)/shard_map/ppermute | solution.py:189
  94.6 4.6 copy-start.31
  99.1 0.7 copy-start.33
  99.1 0.7 copy-start.35
  104.7 91.4 %all-gather.14.cloned.1.call-start = ((), (), s32[]{:S(2)}) async-start(), calls=%async_computation.13 | async-start | bytes 5013504 | tf_op jit(solution)/shard_map/all_gather | solution.py:258
  106.7 6.6 %copy-start.22 = (bf16[512]{0:T(512)(128)(2,1)S(1)}, bf16[512]{0:T(512)(128)(2,1)}, u32[]{:S(2)}) copy-start(bf16[512]{0:T(512)(128)(2,1)} %param.27) | copy-start | bytes 3076
  109.0 25.6 %all-to-all-start = ((bf16[128,8,512]{0,2,1:T(8,128)(2,1)}), bf16[128,8,512]{0,2,1:T(8,128)(2,1)}, u32[]{:S(2)}, u32[]{:S(2)}) async-start(bf16[128,8,512]{0,2,1:T(8,128)(2,1)} %bitcast.227), calls=%async_computation | async-start | bytes 2097152 | tf_op jit(solution)/shard_map/all_to_all | solution.py:256
  113.2 147.4 %reduce-scatter.7.cloned.1.call-start = ((), (), s32[]{:S(2)}) async-start(), calls=%async_computation.9 | async-start | bytes 5013504 | tf_op jit(solution)/shard_map/reduce_scatter | solution.py:297
  196.1 6.9 %copy-start.19 = (bf16[8,128,512]{2,1,0:T(8,128)(2,1)S(1)}, bf16[8,128,512]{2,1,0:T(8,128)(2,1)}, u32[]{:S(2)}) copy-start(bf16[8,128,512]{2,1,0:T(8,128)(2,1)} %copy.46) | copy-start | bytes 3145732
  203.0 4.8 copy-start.37
  207.8 109.2 %reduce-scatter.5.cloned.1.call-start = ((), (), s32[]{:S(2)}) async-start(), calls=%async_computation.8 | async-start | bytes 5013504 | tf_op jit(solution)/shard_map/reduce_scatter | solution.py:297
  214.0 1.1 copy-start.6
  214.0 181.8 %reduce-scatter.11.cloned.1.call-start = ((), (), s32[]{:S(2)}) async-start(), calls=%async_computation.11 | async-start | bytes 2654208 | tf_op jit(solution)/shard_map/reduce_scatter | solution.py:342
  317.0 2.8 copy-start.30
  319.8 6.9 %copy-start.10 = (f32[288,1024]{1,0:T(8,128)}, f32[288,1024]{1,0:T(8,128)S(1)}, u32[]{:S(2)}) copy-start(f32[288,1024]{1,0:T(8,128)S(1)} %get-tuple-element.63) | copy-start | bytes 3538948
  319.8 2.2 copy-start.9
  319.8 6.9 %copy-start.21 = (bf16[1,288,256]{2,1,0:T(8,128)(2,1)S(1)}, bf16[1,288,256]{2,1,0:T(8,128)(2,1)}, u32[]{:S(2)}) copy-start(bf16[1,288,256]{2,1,0:T(8,128)(2,1)} %get-tuple-element.78) | copy-start | bytes 442372
  319.8 6.8 %copy-start.32 = (bf16[1,288,256]{2,1,0:T(8,128)(2,1)S(1)}, bf16[1,288,256]{2,1,0:T(8,128)(2,1)}, u32[]{:S(2)}) copy-start(bf16[1,288,256]{2,1,0:T(8,128)(2,1)} %copy-done.31) | copy-start | bytes 442372
  319.8 6.8 %copy-start.34 = (bf16[1,288,256]{2,1,0:T(8,128)(2,1)S(1)}, bf16[1,288,256]{2,1,0:T(8,128)(2,1)}, u32[]{:S(2)}) copy-start(bf16[1,288,256]{2,1,0:T(8,128)(2,1)} %copy-done.33) | copy-start | bytes 442372
  319.9 6.8 %copy-start.36 = (bf16[1,288,256]{2,1,0:T(8,128)(2,1)S(1)}, bf16[1,288,256]{2,1,0:T(8,128)(2,1)}, u32[]{:S(2)}) copy-start(bf16[1,288,256]{2,1,0:T(8,128)(2,1)} %copy-done.35) | copy-start | bytes 442372
  322.2 10.9 %collective-permute-start.8 = (bf16[1,288,256]{2,1,0:T(8,128)(2,1)S(1)}, bf16[1,288,256]{2,1,0:T(8,128)(2,1)S(1)}, u32[]{:S(2)}, u32[]{:S(2)}) collective-permute-start(bf16[1,288,256]{2,1,0:T(8,128)(2,1)S(1)} %get-tuple-element.75), channel_id=1, source_target_pairs={{0,3},{1,0},{2,1},{3,2},{4,7},{5,4},{6,5},{7,6},{8,11},{9,8},{10,9... | collective-permute-start | bytes 442376 | tf_op jit(solution)/shard_map/ppermute | solution.py:189
  325.6 12.7 %collective-permute-start.7 = (bf16[1,288,256]{2,1,0:T(8,128)(2,1)S(1)}, bf16[1,288,256]{2,1,0:T(8,128)(2,1)S(1)}, u32[]{:S(2)}, u32[]{:S(2)}) collective-permute-start(bf16[1,288,256]{2,1,0:T(8,128)(2,1)S(1)} %get-tuple-element.76), channel_id=1, source_target_pairs={{0,2},{1,3},{2,0},{3,1},{4,6},{5,7},{6,4},{7,5},{8,10},{9,11},{10,... | collective-permute-start | bytes 442376 | tf_op jit(solution)/shard_map/ppermute | solution.py:189
  325.6 12.7 %collective-permute-start.6 = (bf16[1,288,256]{2,1,0:T(8,128)(2,1)S(1)}, bf16[1,288,256]{2,1,0:T(8,128)(2,1)S(1)}, u32[]{:S(2)}, u32[]{:S(2)}) collective-permute-start(bf16[1,288,256]{2,1,0:T(8,128)(2,1)S(1)} %get-tuple-element.77), channel_id=1, source_target_pairs={{0,1},{1,2},{2,3},{3,0},{4,5},{5,6},{6,7},{7,4},{8,9},{9,10},{10,1... | collective-permute-start | bytes 442376 | tf_op jit(solution)/shard_map/ppermute | solution.py:189
  332.6 150.7 %reduce-scatter.9.cloned.1.call-start = ((), (), s32[]{:S(2)}) async-start(), calls=%async_computation.10 | async-start | bytes 1990656 | tf_op jit(solution)/shard_map/reduce_scatter | solution.py:372
  338.3 1.6 copy-start.3
  356.0 1.1 copy-start.8
  356.0 1.2 copy-start.14
  357.2 6.7 %copy-start.16 = (bf16[1,288,1024]{2,1,0:T(8,128)(2,1)S(1)}, bf16[1,288,1024]{2,1,0:T(8,128)(2,1)}, u32[]{:S(2)}) copy-start(bf16[1,288,1024]{2,1,0:T(8,128)(2,1)} %copy-done.15) | copy-start | bytes 1769476
  367.6 2.4 copy-start.38
  375.8 18.9 %all-to-all-start.1 = ((bf16[8,128,512]{2,1,0:T(8,128)(2,1)}), bf16[8,128,512]{2,1,0:T(8,128)(2,1)S(1)}, u32[]{:S(2)}, u32[]{:S(2)}) async-start(bf16[8,128,512]{2,1,0:T(8,128)(2,1)} %bitcast.59), calls=%async_computation.5 | async-start | bytes 2097152 | tf_op jit(solution)/shard_map/all_to_all | solution.py:313
  379.4 169.4 %all-reduce.11.cloned.1.call-start = ((), (), s32[]{:S(2)}) async-start(), calls=%async_computation.14 | async-start | bytes 4849664 | tf_op jit(solution)/shard_map/psum | solution.py:345
  394.7 2.0 copy-start.12
  395.9 5.9 %copy-start.5 = (bf16[1,260,1024]{2,1,0:T(8,128)(2,1)S(1)}, bf16[1,260,1024]{2,1,0:T(8,128)(2,1)}, u32[]{:S(2)}) copy-start(bf16[1,260,1024]{2,1,0:T(8,128)(2,1)} %param.15) | copy-start | bytes 1597444
  396.7 5.5 copy-start.17
  396.9 23.6 %collective-permute-start.9 = (bf16[1,288,1024]{2,1,0:T(8,128)(2,1)S(1)}, bf16[1,288,1024]{2,1,0:T(8,128)(2,1)S(1)}, u32[]{:S(2)}, u32[]{:S(2)}) collective-permute-start(bf16[1,288,1024]{2,1,0:T(8,128)(2,1)S(1)} %get-tuple-element.66), channel_id=1, source_target_pairs={{0,3},{1,0},{2,1},{3,2},{4,7},{5,4},{6,5},{7,6},{8,11},{9,8},{10,9... | collective-permute-start | bytes 1769480 | tf_op jit(solution)/shard_map/ppermute | solution.py:189
  398.2 30.0 %collective-permute-start.11 = (bf16[1,288,1024]{2,1,0:T(8,128)(2,1)S(1)}, bf16[1,288,1024]{2,1,0:T(8,128)(2,1)S(1)}, u32[]{:S(2)}, u32[]{:S(2)}) collective-permute-start(bf16[1,288,1024]{2,1,0:T(8,128)(2,1)S(1)} %get-tuple-element.67), channel_id=1, source_target_pairs={{0,1},{1,2},{2,3},{3,0},{4,5},{5,6},{6,7},{7,4},{8,9},{9,10},{10,1... | collective-permute-start | bytes 1769480 | tf_op jit(solution)/shard_map/ppermute | solution.py:189
  399.0 82.4 %collective-permute-start.10 = (bf16[1,288,1024]{2,1,0:T(8,128)(2,1)S(1)}, bf16[1,288,1024]{2,1,0:T(8,128)(2,1)S(1)}, u32[]{:S(2)}, u32[]{:S(2)}) collective-permute-start(bf16[1,288,1024]{2,1,0:T(8,128)(2,1)S(1)} %get-tuple-element.68), channel_id=1, source_target_pairs={{0,2},{1,3},{2,0},{3,1},{4,6},{5,7},{6,4},{7,5},{8,10},{9,11},{10,... | collective-permute-start | bytes 1769480 | tf_op jit(solution)/shard_map/ppermute | solution.py:189
  403.1 79.0 %copy-start.11 = (f32[288,1024]{1,0:T(8,128)S(1)}, f32[288,1024]{1,0:T(8,128)}, u32[]{:S(2)}) copy-start(f32[288,1024]{1,0:T(8,128)} %copy-done.10) | copy-start | bytes 3538948
  548.7 4.3 copy-start.20
  550.6 4.5 copy-start.18
  553.0 3.6 copy-start.1
Sparse Core Ops, SparseCore 0:
  10.6 28.5 all-gather.7
  41.1 27.8 all-gather.9
  104.8 51.6 all-gather.11
  158.2 37.8 all-gather.13
  207.9 52.6 reduce-scatter.6
  264.3 52.6 reduce-scatter.4
  332.8 41.8 reduce-scatter.10
  379.0 39.3 reduce-scatter.8
  421.7 126.9 all-reduce.10

commit v3 on v2

--- a/solution.py
+++ b/solution.py
@@ -189,6 +189,18 @@
     return lax.ppermute(block, "seq", pairs)
 
 
+def exchange_sum(blocks):
+    owners = blocks.shape[0]
+    mine = lax.axis_index("dp")
+    total = lax.dynamic_index_in_dim(blocks, mine, 0, keepdims=False).astype(jnp.float32)
+    for step in range(1, owners):
+        target = lax.rem(mine + step, owners)
+        block = lax.dynamic_index_in_dim(blocks, target, 0, keepdims=False)
+        pairs = [(place, (place + step) % owners) for place in range(owners)]
+        total += lax.ppermute(block, "dp", pairs).astype(jnp.float32)
+    return total
+
+
 def turned(array, by):
     return lax.dynamic_slice_in_dim(jnp.concatenate([array, array]), by, array.shape[0])
 
@@ -255,6 +267,7 @@
     out_full = turned(lax.all_gather(w_out, "dp", axis=0, tiled=True), my_seq * local_width)
     up_cols = lax.all_to_all(w_up, "dp", split_axis=1, concat_axis=0, tiled=True)
     cot_mine = pad_rows(cotangent, mlp_len, 1).reshape(images * mlp_len, width)
+    slots, cot_mine, up_cols = lax.optimization_barrier((slots, cot_mine, up_cols))
     cot_all = lax.all_gather(cot_mine, "dp", axis=0, tiled=True)
 
     place = jnp.arange(seq_len)
@@ -302,11 +315,8 @@
     activated = gelu_value(preact).astype(bf16)
     d_preact = d_act * gelu_slope(preact)
     grad_hidden = d_preact.astype(bf16)
-    d_second = from_mlp(scatter(against(grad_hidden, up_cols).astype(bf16)))
+    d_second = scatter(against(grad_hidden, up_cols).astype(bf16))
     mlp_part = jnp.dot(activated, w_down, preferred_element_type=f32).astype(bf16)
-    mlp_sum = from_mlp(scatter(mlp_part))
-    outputs = (residual + mlp_sum + down_bias.astype(f32)).astype(bf16)
-    outputs = outputs.reshape(images, padded, width)[:, :shard_len]
     bias_up = jnp.sum(d_preact, axis=0)
     bias_row = jnp.pad(bias_up[None, :], ((0, 15), (0, width - hidden_local)))
     grad_down = jnp.concatenate([outer_sum(activated, cot_all), bias_row]).astype(bf16)
@@ -317,10 +327,11 @@
         concat_axis=1,
         tiled=True,
     )
+    d_second, mlp_part, grad_down, grad_up = lax.optimization_barrier(
+        (d_second, mlp_part, grad_down, grad_up)
+    )
+    d_second = from_mlp(d_second)
     grad_down, grad_up = lax.psum((grad_down, grad_up), "seq")
-    own_up = grad_down[hidden_local, :hidden_local].astype(f32)
-    grad_down = grad_down[:hidden_local].astype(f32)
-    grad_up = grad_up.astype(f32)
 
     cot_rows = from_mlp(cot_mine)
     bias_down = jnp.sum(cot_rows, axis=0)
@@ -334,25 +345,30 @@
     ]
     grads = [grads[0]] + [shift(grads[k], k) for k in range(1, groups)]
     d_heads = jnp.concatenate(grads, axis=1).reshape(images * seq_len, local_width)
+    d_heads, mlp_part = lax.optimization_barrier((d_heads, mlp_part))
+    mlp_sum = from_mlp(exchange_sum(mlp_part.reshape(owners, images * mlp_len, width)))
+    outputs = (residual + mlp_sum + down_bias.astype(f32)).astype(bf16)
+    outputs = outputs.reshape(images, padded, width)[:, :shard_len]
     bias_out = jnp.sum(d_residual, axis=0)
     grad_out = turned(
         outer_sum(merged_rows, res_bf).astype(bf16), (groups - my_seq) * local_width
     ).reshape(owners, rows_owned, width)
     small = extra_rows((second_gain, second_shift, bias_out, bias_down), owners, width)
-    grad_out = lax.psum_scatter(
-        jnp.concatenate([grad_out, small], axis=1), "dp", scatter_dimension=0, tiled=False
-    )
-    grad_out = lax.psum(grad_out, "seq").astype(f32)
-    small = grad_out[rows_owned, : 4 * rows_owned].reshape(4, rows_owned)
-    own_second_gain, own_second_shift, own_out, own_down = small
-    grad_out = grad_out[:rows_owned]
+    grad_out = jnp.concatenate([grad_out, small], axis=1)
 
     d_proj = jnp.concatenate(
         attention_backward(projected, live, attended, lse, d_heads, images, factor), axis=1
     )
+    d_proj, grad_down, grad_up, grad_out = lax.optimization_barrier(
+        (d_proj, grad_down, grad_up, grad_out)
+    )
+    grad_out = lax.psum_scatter(grad_out, "dp", scatter_dimension=0, tiled=False)
     d_part = against(d_proj, qkv_cols)
     first_gain = jnp.sum(d_part * normed_all, axis=0)
     first_shift = jnp.sum(d_part, axis=0)
+    own_up = grad_down[hidden_local, :hidden_local].astype(f32)
+    grad_down = grad_down[:hidden_local].astype(f32)
+    grad_up = grad_up.astype(f32)
     by_slot = d_part.astype(bf16).reshape(images, groups, padded, width)
     d_first = by_slot[:, 0].astype(f32)
     for k in range(1, groups):
@@ -370,7 +386,13 @@
         [grad_qkv.reshape(owners, rows_owned, 3 * local_width), small], axis=1
     )
     grad_qkv = lax.psum_scatter(grad_qkv, "dp", scatter_dimension=0, tiled=False)
-    grad_qkv = lax.all_gather(grad_qkv, "seq", axis=0, tiled=False).astype(f32)
+    last = jnp.concatenate([grad_out, grad_qkv], axis=1)
+    lasts = jnp.stack([last] + [shift(last, -k) for k in range(1, groups)]).astype(f32)
+    grad_out = jnp.sum(lasts[:, :, :width], axis=0)
+    small = grad_out[rows_owned, : 4 * rows_owned].reshape(4, rows_owned)
+    own_second_gain, own_second_shift, own_out, own_down = small
+    grad_out = grad_out[:rows_owned]
+    grad_qkv = turned(lasts[:, :, width:], groups - my_seq)
     small = jnp.sum(grad_qkv[:, rows_owned], axis=0)
     own_gain = small[:rows_owned]
     own_shift = small[rows_owned : 2 * rows_owned]

time: 573 us -> 557 us (0.972); the launches traced: 563 us -> 554 us
  waiting for transfers between devices: 349 us -> 319 us
  starting transfers between devices: 30.1 us -> 51.1 us
  blocking collectives: 28.9 us -> 18.1 us
    reduce_scatter x2 -> x1, waiting for transfers between devices: 100 us -> 22.6 us  [scatter(): return lax.psum_scatter(blocks, 'dp', scatter_dimension=0, tiled=False)]
    ppermute x0 -> x7, waiting for transfers between devices: none -> 51 us  [exchange_sum(): total += lax.ppermute(block, 'dp', pairs).astype(jnp.float32)]
    all_to_all x1, waiting for transfers between devices: 21.3 us -> 0.01 us  [shards(): lax.all_to_all(w_up, 'dp', split_axis=1, concat_axis=0, tiled=True)]
    all_gather x1 -> x0, blocking collectives: 20 us -> none  [shards(): grad_qkv = lax.all_gather(grad_qkv, 'seq', axis=0, tiled=False).astype(f32)]
    psum x1, waiting for transfers between devices: 38.4 us -> 55.3 us  [shards(): grad_down, grad_up = lax.psum((grad_down, grad_up), 'seq')]
    all_gather x1, waiting for transfers between devices: 19.7 us -> 35.2 us  [shards(): lax.all_gather(to_mlp(pre_two.astype(bf16)), 'dp', axis=0, tiled=True)]
    ppermute x12 -> x15, starting transfers between devices: 21.3 us -> 35.6 us  [shift(): return lax.ppermute(block, 'seq', pairs)]
    ppermute x12 -> x15, waiting for transfers between devices: 129 us -> 117 us  [shift(): return lax.ppermute(block, 'seq', pairs)]
  transfers between devices with their start and end apart: 23 -> 32, of which waited for: 15 -> 17; matrix products, arithmetic and copies ran while one was open for 13% -> 13% of each run, Pallas kernels for 5% -> 5%
where the time goes in v3:
time: 557 us; the launch traced here: 554 us
  waiting for transfers between devices  319 us (57%)
  matrix products  62.4 us (11%)
  starting transfers between devices  51.1 us (9%)
  local copies, waits for them, and re-layouts  32 us (6%)
  other arithmetic  27.6 us (5%)
  Pallas kernels  27.5 us (5%)
  blocking collectives  18.1 us (3%)
  between operations  15.9 us (3%)
    ppermute x15, waiting for transfers between devices, shift(): return lax.ppermute(block, 'seq', pairs)  117 us
    psum x1, waiting for transfers between devices, shards(): grad_down, grad_up = lax.psum((grad_down, grad_up), 'seq')  55.3 us
    ppermute x7, waiting for transfers between devices, exchange_sum(): total += lax.ppermute(block, 'dp', pairs).astype(jnp.float32)  51 us
    ppermute x15, starting transfers between devices, shift(): return lax.ppermute(block, 'seq', pairs)  35.6 us
    all_gather x1, waiting for transfers between devices, shards(): lax.all_gather(to_mlp(pre_two.astype(bf16)), 'dp', axis=0, tiled=True)  35.2 us
    all_gather x1, waiting for transfers between devices, shards(): cot_all = lax.all_gather(cot_mine, 'dp', axis=0, tiled=True)  31.1 us
    reduce_scatter x1, waiting for transfers between devices, scatter(): return lax.psum_scatter(blocks, 'dp', scatter_dimension=0, tiled=False)  22.6 us
    dot_general x4, matrix products, against(): lax.dot_general(left_mat, right_mat, (((1,), (1,)), ((), ())), preferred_...  22.1 us
  transfers between devices with their start and end apart: 32, of which 17 were waited for; matrix products, arithmetic and copies ran while one was open for 13% of the time, Pallas kernels for 5%

profile of v3, /device:TPU:0, one launch (start us, length us, event | category | flops | bytes accessed | tf_op | source)
XLA Modules:
  0.0 553.9 jit_solution(2218696306229613768)
XLA Ops:
  7.3 1.6 copy.50
  10.5 3.1 collective-permute-start
  13.6 2.6 collective-permute-start.1
  16.2 1.3 collective-permute-start.2
  17.6 2.3 copy.48
  19.8 4.2 all-to-all-start
  25.6 18.1 %all-gather = bf16[8192]{0:T(1024)(128)(2,1)S(1)} all-gather(bf16[1024]{0:T(1024)(128)(2,1)S(1)} %dynamic-update-slice.6), channel_id=2, replica_groups=mesh['dp'=8,'seq'=4] {'dp'}, dimensions={0}, use_global_device_ids=true | all-gather | bytes 18432 | tf_op jit(solution)/shard_map/all_gather | solution.py:256
  45.8 2.3 copy.49
  48.1 6.4 %collective-permute-done.1 = bf16[1,288,1024]{2,1,0:T(8,128)(2,1)} collective-permute-done((bf16[1,288,1024]{2,1,0:T(8,128)(2,1)S(1)}, bf16[1,288,1024]{2,1,0:T(8,128)(2,1)}, u32[]{:S(2)}, u32[]{:S(2)}) %collective-permute-start.1) | collective-permute-done | bytes 589856 | tf_op jit(solution)/shard_map/ppermute | solution.py:189
  54.5 1.6 convert_reduce_fusion
  56.1 2.1 fusion.8
  58.3 4.2 fusion.16.q_ref.k_ref.v_ref
  62.5 11.3 %attention_forward.1 = (bf16[1152,256]{1,0:T(8,128)(2,1)S(1)}, f32[1,2,2,1152]{3,2,1,0:T(2,128)S(1)}) custom-call(f32[1,1152,1]{2,1,0:T(8,128)S(1)} %fusion.78.live_ref, bf16[1152,768]{1,0:T(8,128)(2,1)S(1)} %fusion.16.q_ref.k_ref.v_ref, bf16[1152,768]{1,0:T(8,128)(2,1)S(1)} %fusion.16.q_ref.k_ref.v_ref, bf16[1152,768]{1,0:T(8,128)(2,1)S(1)} %fusion.16.q_ref.k_ref.v_ref), custom_call_target="tpu_custom_call" | custom-call | flops 1358954496 | bytes 2359296 | tf_op jit(solution)/shard_map/attention_forward/pallas_call | solution.py:148
  74.5 14.2 %collective-permute-start.3 = (bf16[1,288,256]{2,1,0:T(8,128)(2,1)S(1)}, bf16[1,288,256]{2,1,0:T(8,128)(2,1)S(1)}, u32[]{:S(2)}, u32[]{:S(2)}) collective-permute-start(bf16[1,288,256]{2,1,0:T(8,128)(2,1)S(1)} %get-tuple-element.118), channel_id=1, source_target_pairs={{0,3},{1,0},{2,1},{3,2},{4,7},{5,4},{6,5},{7,6},{8,11},{9,8},{10,9... | collective-permute-start | bytes 442376 | tf_op jit(solution)/shard_map/ppermute | solution.py:189
  89.2 3.7 collective-permute-done.3
  92.9 9.4 %collective-permute-done.4 = bf16[1,288,256]{2,1,0:T(8,128)(2,1)S(1)} collective-permute-done((bf16[1,288,256]{2,1,0:T(8,128)(2,1)S(1)}, bf16[1,288,256]{2,1,0:T(8,128)(2,1)S(1)}, u32[]{:S(2)}, u32[]{:S(2)}) %collective-permute-start.4) | collective-permute-done | bytes 147488 | tf_op jit(solution)/shard_map/ppermute | solution.py:189
  103.0 3.4 fusion.124
  109.1 35.2 %all-gather.13.cloned.1.call-done = bf16[1,2176,1024]{2,1,0:T(8,128)(2,1)} async-done(((bf16[1,272,1024]{2,1,0:T(8,128)(2,1)}), bf16[1,2176,1024]{2,1,0:T(8,128)(2,1)}) %all-gather.13.cloned.1.call-update) | async-done | bytes 4456464 | tf_op jit(solution)/shard_map/all_gather | solution.py:312
  144.3 8.5 %multiply_convert_fusion = (bf16[2176,512]{1,0:T(8,128)(2,1)}, f32[2176,512]{1,0:T(8,128)}) fusion(f32[512]{0:T(512)S(1)} %convert_element_type.251, bf16[1024,512]{1,0:T(8,128)(2,1)} %bitcast.267, bf16[1,2176,1024]{2,1,0:T(8,128)(2,1)} %all-gather.13.cloned.1.call-done), kind=kOutput, calls=%fused_computation.23 | convolution fusion | flops 2288386048 | bytes 12191744 | tf_op jit(solution)/shard_map/dot_general | solution.py:314
  152.7 31.1 %all-gather.11.cloned.1.call-done = bf16[2176,1024]{1,0:T(8,128)(2,1)} async-done(((bf16[272,1024]{1,0:T(8,128)(2,1)}), bf16[2176,1024]{1,0:T(8,128)(2,1)}) %all-gather.11.cloned.1.call-update) | async-done | bytes 4456464 | tf_op jit(solution)/shard_map/all_gather | solution.py:271
  183.9 6.9 %fusion.125 = (bf16[512]{0:T(512)(128)(2,1)S(1)}, bf16[2176,512]{1,0:T(8,128)(2,1)S(1)}) fusion(f32[2176,512]{1,0:T(8,128)} %get-tuple-element.136, bf16[2176,1024]{1,0:T(8,128)(2,1)} %all-gather.11.cloned.1.call-done, bf16[512,1024]{1,0:T(8,128)(2,1)S(1)} %copy-done), kind=kOutput, calls=%fused_computation.224 | convolution fusion | flops 2293956096 | bytes 12190720 | tf_op jit(solution)/shard_map/dot_general | solution.py:47
  190.8 4.7 convolution_convert_fusion.1
  196.6 6.6 %fusion.21 = bf16[1024,512]{1,0:T(8,128)(2,1)} fusion(bf16[1,2176,1024]{2,1,0:T(8,128)(2,1)} %all-gather.13.cloned.1.call-done, bf16[2176,512]{1,0:T(8,128)(2,1)} %copy-done.36), kind=kOutput, calls=%fused_computation.46 | convolution fusion | flops 2282225664 | bytes 7733248 | tf_op jit(solution)/shard_map/dot_general | solution.py:53
  203.2 4.3 all-to-all-start.1
  207.7 6.0 %convolution_convert_fusion.4 = bf16[512,1024]{1,0:T(8,128)(2,1)S(1)} fusion(bf16[2176,512]{1,0:T(8,128)(2,1)} %get-tuple-element.135, bf16[2176,1024]{1,0:T(8,128)(2,1)} %all-gather.11.cloned.1.call-done), kind=kOutput, calls=%fused_computation.47 | convolution fusion | flops 2282225664 | bytes 7733248 | tf_op jit(solution)/shard_map/dot_general | solution.py:53
  214.8 4.7 convolution_convert_fusion
  219.5 5.5 all-to-all-done.1
  225.0 2.4 copy.62
  227.3 22.6 %reduce-scatter.4.cloned.1.call-done = bf16[1,272,1024]{2,1,0:T(8,128)(2,1)} async-done(((bf16[8,272,1024]{2,1,0:T(8,128)(2,1)}), bf16[1,272,1024]{2,1,0:T(8,128)(2,1)}) %reduce-scatter.4.cloned.1.call-update) | async-done | bytes 557072 | tf_op jit(solution)/shard_map/reduce_scatter | solution.py:310
  250.0 1.7 fusion.45
  251.8 1.5 fusion.119
  253.5 3.4 fusion.34
  257.7 1.4 collective-permute-start.6
  259.1 2.5 collective-permute-start.7
  261.5 1.4 collective-permute-start.8
  264.3 2.8 fusion.18
  267.1 1.6 pad_maximum_fusion.1
  269.2 9.9 %collective-permute-done.7 = bf16[1,288,256]{2,1,0:T(8,128)(2,1)S(1)} collective-permute-done((bf16[1,288,256]{2,1,0:T(8,128)(2,1)}, bf16[1,288,256]{2,1,0:T(8,128)(2,1)S(1)}, u32[]{:S(2)}, u32[]{:S(2)}) %collective-permute-start.7) | collective-permute-done | bytes 147488 | tf_op jit(solution)/shard_map/ppermute | solution.py:189
  279.1 1.5 copy-done.3
  280.6 16.3 %attention_backward.1 = (bf16[1152,256]{1,0:T(8,128)(2,1)S(1)}, bf16[1152,256]{1,0:T(8,128)(2,1)S(1)}, bf16[1152,256]{1,0:T(8,128)(2,1)S(1)}) custom-call(f32[1,1152,1]{2,1,0:T(8,128)S(1)} %fusion.78.live_ref, bf16[1152,768]{1,0:T(8,128)(2,1)S(1)} %copy-done.3, bf16[1152,768]{1,0:T(8,128)(2,1)S(1)} %copy-done.3, bf16[1152,768]{1,0:T(8,128)(2,1)S(1)} %copy-done.3, ...), custom_call_target="tpu_custom_call" | custom-call | flops 3397386240 | bytes 4718592 | tf_op jit(solution)/shard_map/attention_backward/pallas_call | solution.py:171
  298.2 55.3 %all-reduce.11.cloned.1.call-done = (bf16[528,1024]{1,0:T(8,128)(2,1)}, bf16[128,4096]{1,0:T(8,128)(2,1)}) async-done(((bf16[528,1024]{1,0:T(8,128)(2,1)}, bf16[128,4096]{1,0:T(8,128)(2,1)}), (bf16[528,1024]{1,0:T(8,128)(2,1)}, bf16[128,4096]{1,0:T(8,128)(2,1)})) %all-reduce.11.cloned.1.call-update) | async-done | bytes 2129936 | tf_op jit(solution)/shard_map/psum | solution.py:334
  353.5 5.7 %convolution_convert_fusion.3 = bf16[1024,768]{1,0:T(8,128)(2,1)} fusion(bf16[1152,768]{1,0:T(8,128)(2,1)} %pad_maximum_fusion.2, f32[1024]{0:T(1024)S(1)} %get-tuple-element.125, f32[1024]{0:T(1024)S(1)} %get-tuple-element.126, f32[1152]{0:T(1024)S(1)} %add_rsqrt_fusion, f32[1152]{0:T(1024)S(1)} %broadcast_multiply_fusion, ...), kind=kOutput, calls=%fused_computation.45 | convolution fusion | flops 1828061184 | bytes 5719040 | tf_op jit(solution)/shard_map/dot_general | solution.py:53
  359.6 7.2 %fusion.7 = (bf16[1024]{0:T(1024)(128)(2,1)S(1)}, bf16[1024]{0:T(1024)(128)(2,1)S(1)}, bf16[1152,1024]{1,0:T(8,128)(2,1)}) fusion(f32[1152]{0:T(1024)S(1)} %add_rsqrt_fusion, f32[1152]{0:T(1024)S(1)} %broadcast_multiply_fusion, bf16[1,288,1024]{2,1,0:T(8,128)(2,1)} %collective-permute-done.2, bf16[1,288,1024]{2,1,0:T(8,128)(2,1)} %collective-permute-done.1, ...), kind=kOutput, calls=%fused_computation.14 | convolution fusion | flops 1828452352 | bytes 8074240 | tf_op jit(solution)/shard_map/dot_general | solution.py:47
  369.0 3.7 dynamic-slice_bitcast_fusion.6
  372.8 1.5 collective-permute-start.10
  376.0 1.5 collective-permute-start.13
  377.4 1.5 collective-permute-start.14
  378.9 10.6 %collective-permute-done.10 = bf16[272,1024]{1,0:T(8,128)(2,1)} collective-permute-done((bf16[272,1024]{1,0:T(8,128)(2,1)}, bf16[272,1024]{1,0:T(8,128)(2,1)}, u32[]{:S(2)}, u32[]{:S(2)}) %collective-permute-start.10) | collective-permute-done | bytes 557088 | tf_op jit(solution)/shard_map/ppermute | solution.py:200
  389.6 21.4 %collective-permute-done.11 = bf16[272,1024]{1,0:T(8,128)(2,1)} collective-permute-done((bf16[272,1024]{1,0:T(8,128)(2,1)}, bf16[272,1024]{1,0:T(8,128)(2,1)}, u32[]{:S(2)}, u32[]{:S(2)}) %collective-permute-start.11) | collective-permute-done | bytes 557088 | tf_op jit(solution)/shard_map/ppermute | solution.py:200
  411.3 19.0 %collective-permute-done.13 = bf16[272,1024]{1,0:T(8,128)(2,1)S(1)} collective-permute-done((bf16[272,1024]{1,0:T(8,128)(2,1)}, bf16[272,1024]{1,0:T(8,128)(2,1)S(1)}, u32[]{:S(2)}, u32[]{:S(2)}) %collective-permute-start.13) | collective-permute-done | bytes 557088 | tf_op jit(solution)/shard_map/ppermute | solution.py:200
  430.3 2.3 fusion.58
  432.8 1.6 collective-permute-start.16
  434.4 1.5 collective-permute-start.18
  437.0 1.5 convert_element_type.282
  439.1 1.6 slice_convert_fusion
  440.7 9.6 %collective-permute-done.16 = bf16[1,288,1024]{2,1,0:T(8,128)(2,1)S(1)} collective-permute-done((bf16[1,288,1024]{2,1,0:T(8,128)(2,1)S(1)}, bf16[1,288,1024]{2,1,0:T(8,128)(2,1)S(1)}, u32[]{:S(2)}, u32[]{:S(2)}) %collective-permute-start.16) | collective-permute-done | bytes 589856 | tf_op jit(solution)/shard_map/ppermute | solution.py:189
  450.3 35.5 %collective-permute-done.17 = bf16[1,288,1024]{2,1,0:T(8,128)(2,1)S(1)} collective-permute-done((bf16[1,288,1024]{2,1,0:T(8,128)(2,1)S(1)}, bf16[1,288,1024]{2,1,0:T(8,128)(2,1)S(1)}, u32[]{:S(2)}, u32[]{:S(2)}) %collective-permute-start.17) | collective-permute-done | bytes 589856 | tf_op jit(solution)/shard_map/ppermute | solution.py:189
  487.8 3.5 collective-permute-start.20
  491.2 1.9 collective-permute-start.21
  494.4 7.1 %collective-permute-done.19 = bf16[144,1792]{1,0:T(8,128)(2,1)S(1)} collective-permute-done((bf16[144,1792]{1,0:T(8,128)(2,1)S(1)}, bf16[144,1792]{1,0:T(8,128)(2,1)S(1)}, u32[]{:S(2)}, u32[]{:S(2)}) %collective-permute-start.19) | collective-permute-done | bytes 516128 | tf_op jit(solution)/shard_map/ppermute | solution.py:189
  501.5 34.6 %collective-permute-done.20 = bf16[144,1792]{1,0:T(8,128)(2,1)S(1)} collective-permute-done((bf16[144,1792]{1,0:T(8,128)(2,1)S(1)}, bf16[144,1792]{1,0:T(8,128)(2,1)S(1)}, u32[]{:S(2)}, u32[]{:S(2)}) %collective-permute-start.20) | collective-permute-done | bytes 516128 | tf_op jit(solution)/shard_map/ppermute | solution.py:189
  539.4 1.6 copy.59
  541.0 2.8 copy.60
  543.8 3.0 copy.61
  (189 shorter events, 28.6 us)
Async XLA Ops:
  7.2 176.7 %copy-start = (bf16[512,1024]{1,0:T(8,128)(2,1)S(1)}, bf16[512,1024]{1,0:T(8,128)(2,1)}, u32[]{:S(2)}) copy-start(bf16[512,1024]{1,0:T(8,128)(2,1)} %param.28) | copy-start | bytes 3145732
  7.2 3.2 copy-start.4
  7.2 51.1 %all-gather.7.cloned.1.call-start = ((), (), s32[]{:S(2)}) async-start(), calls=%async_computation.5 | async-start | bytes 1769472 | tf_op jit(solution)/shard_map/all_gather | solution.py:266
  9.6 92.7 %all-gather.9.cloned.1.call-start = ((), (), s32[]{:S(2)}) async-start(), calls=%async_computation.6 | async-start | bytes 2359296 | tf_op jit(solution)/shard_map/all_gather | solution.py:267
  10.4 47.9 %copy-start.8 = (bf16[1,288,1024]{2,1,0:T(8,128)(2,1)}, bf16[1,288,1024]{2,1,0:T(8,128)(2,1)S(1)}, u32[]{:S(2)}) copy-start(bf16[1,288,1024]{2,1,0:T(8,128)(2,1)S(1)} %pad.39) | copy-start | bytes 1769476
  10.4 13.7 %copy-start.23 = (bf16[128]{0:T(256)(128)(2,1)S(1)}, bf16[128]{0:T(256)(128)(2,1)}, u32[]{:S(2)}) copy-start(bf16[128]{0:T(256)(128)(2,1)} %param.18) | copy-start | bytes 772
  10.5 13.9 %copy-start.24 = (bf16[128]{0:T(256)(128)(2,1)S(1)}, bf16[128]{0:T(256)(128)(2,1)}, u32[]{:S(2)}) copy-start(bf16[128]{0:T(256)(128)(2,1)} %param.19) | copy-start | bytes 772
  10.5 14.1 %copy-start.25 = (bf16[128]{0:T(256)(128)(2,1)S(1)}, bf16[128]{0:T(256)(128)(2,1)}, u32[]{:S(2)}) copy-start(bf16[128]{0:T(256)(128)(2,1)} %param.23) | copy-start | bytes 772
  10.5 14.3 %copy-start.26 = (bf16[128]{0:T(256)(128)(2,1)S(1)}, bf16[128]{0:T(256)(128)(2,1)}, u32[]{:S(2)}) copy-start(bf16[128]{0:T(256)(128)(2,1)} %param.24) | copy-start | bytes 772
  10.5 14.5 %copy-start.27 = (bf16[128]{0:T(256)(128)(2,1)S(1)}, bf16[128]{0:T(256)(128)(2,1)}, u32[]{:S(2)}) copy-start(bf16[128]{0:T(256)(128)(2,1)} %param.25) | copy-start | bytes 772
  10.5 14.7 %copy-start.28 = (bf16[128]{0:T(256)(128)(2,1)S(1)}, bf16[128]{0:T(256)(128)(2,1)}, u32[]{:S(2)}) copy-start(bf16[128]{0:T(256)(128)(2,1)} %param.29) | copy-start | bytes 772
  10.5 14.9 %copy-start.29 = (bf16[256]{0:T(256)(128)(2,1)S(1)}, bf16[256]{0:T(256)(128)(2,1)}, u32[]{:S(2)}) copy-start(bf16[256]{0:T(256)(128)(2,1)} %param.21) | copy-start | bytes 1540
  10.5 34.0 %copy-start.20 = (bf16[1,260,1024]{2,1,0:T(8,128)(2,1)S(1)}, bf16[1,260,1024]{2,1,0:T(8,128)(2,1)}, u32[]{:S(2)}) copy-start(bf16[1,260,1024]{2,1,0:T(8,128)(2,1)} %param.16) | copy-start | bytes 1597444
  10.5 37.6 %collective-permute-start = (bf16[1,288,1024]{2,1,0:T(8,128)(2,1)S(1)}, bf16[1,288,1024]{2,1,0:T(8,128)(2,1)S(1)}, u32[]{:S(2)}, u32[]{:S(2)}) collective-permute-start(bf16[1,288,1024]{2,1,0:T(8,128)(2,1)S(1)} %pad.39), channel_id=1, source_target_pairs={{0,1},{1,2},{2,3},{3,0},{4,5},{5,6},{6,7},{7,4},{8,9},{9,10},{10,1... | collective-permute-start | bytes 1769480 | tf_op jit(solution)/shard_map/ppermute | solution.py:189
  13.6 40.9 %collective-permute-start.1 = (bf16[1,288,1024]{2,1,0:T(8,128)(2,1)S(1)}, bf16[1,288,1024]{2,1,0:T(8,128)(2,1)}, u32[]{:S(2)}, u32[]{:S(2)}) collective-permute-start(bf16[1,288,1024]{2,1,0:T(8,128)(2,1)S(1)} %pad.39), channel_id=1, source_target_pairs={{0,2},{1,3},{2,0},{3,1},{4,6},{5,7},{6,4},{7,5},{8,10},{9,11},{10,... | collective-permute-start | bytes 1769480 | tf_op jit(solution)/shard_map/ppermute | solution.py:189
  16.2 38.3 %collective-permute-start.2 = (bf16[1,288,1024]{2,1,0:T(8,128)(2,1)S(1)}, bf16[1,288,1024]{2,1,0:T(8,128)(2,1)}, u32[]{:S(2)}, u32[]{:S(2)}) collective-permute-start(bf16[1,288,1024]{2,1,0:T(8,128)(2,1)S(1)} %pad.39), channel_id=1, source_target_pairs={{0,3},{1,0},{2,1},{3,2},{4,7},{5,4},{6,5},{7,6},{8,11},{9,8},{10,9... | collective-permute-start | bytes 1769480 | tf_op jit(solution)/shard_map/ppermute | solution.py:189
  19.8 26.0 %all-to-all-start = ((bf16[128,8,512]{0,2,1:T(8,128)(2,1)}), bf16[128,8,512]{0,2,1:T(8,128)(2,1)}, u32[]{:S(2)}, u32[]{:S(2)}) async-start(bf16[128,8,512]{0,2,1:T(8,128)(2,1)} %bitcast.3), calls=%async_computation | async-start | bytes 2097152 | tf_op jit(solution)/shard_map/all_to_all | solution.py:268
  24.1 120.2 %all-gather.13.cloned.1.call-start = ((), (), s32[]{:S(2)}) async-start(), calls=%async_computation.11 | async-start | bytes 5013504 | tf_op jit(solution)/shard_map/all_gather | solution.py:312
  48.1 10.2 %copy-start.14 = (bf16[1,288,1024]{2,1,0:T(8,128)(2,1)}, bf16[1,288,1024]{2,1,0:T(8,128)(2,1)S(1)}, u32[]{:S(2)}) copy-start(bf16[1,288,1024]{2,1,0:T(8,128)(2,1)S(1)} %collective-permute-done) | copy-start | bytes 1769476
  62.5 11.3 %copy-start.2 = (bf16[1152,768]{1,0:T(8,128)(2,1)}, bf16[1152,768]{1,0:T(8,128)(2,1)S(1)}, u32[]{:S(2)}) copy-start(bf16[1152,768]{1,0:T(8,128)(2,1)S(1)} %fusion.16.q_ref.k_ref.v_ref) | copy-start | bytes 5308420
  74.5 18.5 %collective-permute-start.3 = (bf16[1,288,256]{2,1,0:T(8,128)(2,1)S(1)}, bf16[1,288,256]{2,1,0:T(8,128)(2,1)S(1)}, u32[]{:S(2)}, u32[]{:S(2)}) collective-permute-start(bf16[1,288,256]{2,1,0:T(8,128)(2,1)S(1)} %get-tuple-element.118), channel_id=1, source_target_pairs={{0,3},{1,0},{2,1},{3,2},{4,7},{5,4},{6,5},{7,6},{8,11},{9,8},{10,9... | collective-permute-start | bytes 442376 | tf_op jit(solution)/shard_map/ppermute | solution.py:189
  88.6 13.7 %collective-permute-start.4 = (bf16[1,288,256]{2,1,0:T(8,128)(2,1)S(1)}, bf16[1,288,256]{2,1,0:T(8,128)(2,1)S(1)}, u32[]{:S(2)}, u32[]{:S(2)}) collective-permute-start(bf16[1,288,256]{2,1,0:T(8,128)(2,1)S(1)} %get-tuple-element.117), channel_id=1, source_target_pairs={{0,2},{1,3},{2,0},{3,1},{4,6},{5,7},{6,4},{7,5},{8,10},{9,11},{10,... | collective-permute-start | bytes 442376 | tf_op jit(solution)/shard_map/ppermute | solution.py:189
  89.1 13.3 %collective-permute-start.5 = (bf16[1,288,256]{2,1,0:T(8,128)(2,1)S(1)}, bf16[1,288,256]{2,1,0:T(8,128)(2,1)S(1)}, u32[]{:S(2)}, u32[]{:S(2)}) collective-permute-start(bf16[1,288,256]{2,1,0:T(8,128)(2,1)S(1)} %get-tuple-element.116), channel_id=1, source_target_pairs={{0,1},{1,2},{2,3},{3,0},{4,5},{5,6},{6,7},{7,4},{8,9},{9,10},{10,1... | collective-permute-start | bytes 442376 | tf_op jit(solution)/shard_map/ppermute | solution.py:189
  92.9 9.4 %copy-start.30 = (bf16[1,288,256]{2,1,0:T(8,128)(2,1)}, bf16[1,288,256]{2,1,0:T(8,128)(2,1)S(1)}, u32[]{:S(2)}) copy-start(bf16[1,288,256]{2,1,0:T(8,128)(2,1)S(1)} %collective-permute-done.3) | copy-start | bytes 442372
  107.9 76.0 %all-gather.11.cloned.1.call-start = ((), (), s32[]{:S(2)}) async-start(), calls=%async_computation.7 | async-start | bytes 5013504 | tf_op jit(solution)/shard_map/all_gather | solution.py:271
  108.5 141.5 %reduce-scatter.4.cloned.1.call-start = ((), (), s32[]{:S(2)}) async-start(), calls=%async_computation.8 | async-start | bytes 5013504 | tf_op jit(solution)/shard_map/reduce_scatter | solution.py:310
  183.9 6.9 %copy-start.18 = (bf16[8,128,512]{2,1,0:T(8,128)(2,1)S(1)}, bf16[8,128,512]{2,1,0:T(8,128)(2,1)}, u32[]{:S(2)}) copy-start(bf16[8,128,512]{2,1,0:T(8,128)(2,1)} %copy.49) | copy-start | bytes 3145732
  190.8 4.7 copy-start.36
  203.2 21.7 %all-to-all-start.1 = ((bf16[8,128,512]{2,1,0:T(8,128)(2,1)}), bf16[8,128,512]{2,1,0:T(8,128)(2,1)}, u32[]{:S(2)}, u32[]{:S(2)}) async-start(bf16[8,128,512]{2,1,0:T(8,128)(2,1)} %bitcast.269), calls=%async_computation.2 | async-start | bytes 2097152 | tf_op jit(solution)/shard_map/all_to_all | solution.py:323
  207.5 146.0 %all-reduce.11.cloned.1.call-start = ((), (), s32[]{:S(2)}) async-start(), calls=%async_computation.12 | async-start | bytes 4259840 | tf_op jit(solution)/shard_map/psum | solution.py:334
  207.7 7.1 %copy-start.37 = (bf16[2176,512]{1,0:T(8,128)(2,1)S(1)}, bf16[2176,512]{1,0:T(8,128)(2,1)}, u32[]{:S(2)}) copy-start(bf16[2176,512]{1,0:T(8,128)(2,1)} %get-tuple-element.135) | copy-start | bytes 6684676
  225.0 26.8 %copy-start.6 = (bf16[272,1024]{1,0:T(8,128)(2,1)S(1)}, bf16[272,1024]{1,0:T(8,128)(2,1)}, u32[]{:S(2)}) copy-start(bf16[272,1024]{1,0:T(8,128)(2,1)} %pad_bitcast_fusion) | copy-start | bytes 1671172
  253.4 233.1 %reduce-scatter.8.cloned.1.call-start = ((), (), s32[]{:S(2)}) async-start(), calls=%async_computation.10 | async-start | bytes 1990656 | tf_op jit(solution)/shard_map/reduce_scatter | solution.py:388
  253.4 9.5 %copy-start.11 = (f32[288,1024]{1,0:T(8,128)S(1)}, f32[288,1024]{1,0:T(8,128)}, u32[]{:S(2)}) copy-start(f32[288,1024]{1,0:T(8,128)} %get-tuple-element.95) | copy-start | bytes 3538948
  253.5 9.5 %copy-start.21 = (bf16[1,288,256]{2,1,0:T(8,128)(2,1)S(1)}, bf16[1,288,256]{2,1,0:T(8,128)(2,1)}, u32[]{:S(2)}) copy-start(bf16[1,288,256]{2,1,0:T(8,128)(2,1)} %get-tuple-element.115) | copy-start | bytes 442372
  253.5 9.5 %copy-start.31 = (bf16[1,288,256]{2,1,0:T(8,128)(2,1)S(1)}, bf16[1,288,256]{2,1,0:T(8,128)(2,1)}, u32[]{:S(2)}) copy-start(bf16[1,288,256]{2,1,0:T(8,128)(2,1)} %copy-done.30) | copy-start | bytes 442372
  253.5 9.5 %copy-start.33 = (bf16[1,288,256]{2,1,0:T(8,128)(2,1)S(1)}, bf16[1,288,256]{2,1,0:T(8,128)(2,1)}, u32[]{:S(2)}) copy-start(bf16[1,288,256]{2,1,0:T(8,128)(2,1)} %copy-done.32) | copy-start | bytes 442372
  253.5 9.5 %copy-start.35 = (bf16[1,288,256]{2,1,0:T(8,128)(2,1)S(1)}, bf16[1,288,256]{2,1,0:T(8,128)(2,1)}, u32[]{:S(2)}) copy-start(bf16[1,288,256]{2,1,0:T(8,128)(2,1)} %copy-done.34) | copy-start | bytes 442372
  257.7 11.5 %collective-permute-start.6 = (bf16[1,288,256]{2,1,0:T(8,128)(2,1)}, bf16[1,288,256]{2,1,0:T(8,128)(2,1)S(1)}, u32[]{:S(2)}, u32[]{:S(2)}) collective-permute-start(bf16[1,288,256]{2,1,0:T(8,128)(2,1)} %get-tuple-element.114), channel_id=1, source_target_pairs={{0,1},{1,2},{2,3},{3,0},{4,5},{5,6},{6,7},{7,4},{8,9},{9,10},{10,1... | collective-permute-start | bytes 442376 | tf_op jit(solution)/shard_map/ppermute | solution.py:189
  259.1 20.0 %collective-permute-start.7 = (bf16[1,288,256]{2,1,0:T(8,128)(2,1)}, bf16[1,288,256]{2,1,0:T(8,128)(2,1)S(1)}, u32[]{:S(2)}, u32[]{:S(2)}) collective-permute-start(bf16[1,288,256]{2,1,0:T(8,128)(2,1)} %get-tuple-element.113), channel_id=1, source_target_pairs={{0,2},{1,3},{2,0},{3,1},{4,6},{5,7},{6,4},{7,5},{8,10},{9,11},{10,... | collective-permute-start | bytes 442376 | tf_op jit(solution)/shard_map/ppermute | solution.py:189
  261.5 17.5 %collective-permute-start.8 = (bf16[1,288,256]{2,1,0:T(8,128)(2,1)}, bf16[1,288,256]{2,1,0:T(8,128)(2,1)S(1)}, u32[]{:S(2)}, u32[]{:S(2)}) collective-permute-start(bf16[1,288,256]{2,1,0:T(8,128)(2,1)} %get-tuple-element.112), channel_id=1, source_target_pairs={{0,3},{1,0},{2,1},{3,2},{4,7},{5,4},{6,5},{7,6},{8,11},{9,8},{10,9... | collective-permute-start | bytes 442376 | tf_op jit(solution)/shard_map/ppermute | solution.py:189
  296.9 56.6 %copy-start.9 = (bf16[1,288,1024]{2,1,0:T(8,128)(2,1)S(1)}, bf16[1,288,1024]{2,1,0:T(8,128)(2,1)}, u32[]{:S(2)}) copy-start(bf16[1,288,1024]{2,1,0:T(8,128)(2,1)} %copy-done.8) | copy-start | bytes 1769476
  296.9 56.6 %copy-start.15 = (bf16[1,288,1024]{2,1,0:T(8,128)(2,1)S(1)}, bf16[1,288,1024]{2,1,0:T(8,128)(2,1)}, u32[]{:S(2)}) copy-start(bf16[1,288,1024]{2,1,0:T(8,128)(2,1)} %copy-done.14) | copy-start | bytes 1769476
  353.5 5.7 %copy-start.7 = (bf16[1152,768]{1,0:T(8,128)(2,1)S(1)}, bf16[1152,768]{1,0:T(8,128)(2,1)}, u32[]{:S(2)}) copy-start(bf16[1152,768]{1,0:T(8,128)(2,1)} %pad_maximum_fusion.2) | copy-start | bytes 5308420
  359.6 7.2 %copy-start.16 = (bf16[1024,768]{1,0:T(8,128)(2,1)S(1)}, bf16[1024,768]{1,0:T(8,128)(2,1)}, u32[]{:S(2)}) copy-start(bf16[1024,768]{1,0:T(8,128)(2,1)} %convolution_convert_fusion.3) | copy-start | bytes 4718596
  368.2 118.3 %reduce-scatter.6.cloned.1.call-start = ((), (), s32[]{:S(2)}) async-start(), calls=%async_computation.9 | async-start | bytes 2654208 | tf_op jit(solution)/shard_map/reduce_scatter | solution.py:365
  369.0 5.9 %copy-start.5 = (bf16[1,260,1024]{2,1,0:T(8,128)(2,1)S(1)}, bf16[1,260,1024]{2,1,0:T(8,128)(2,1)}, u32[]{:S(2)}) copy-start(bf16[1,260,1024]{2,1,0:T(8,128)(2,1)} %param.15) | copy-start | bytes 1597444
  372.8 16.8 %collective-permute-start.10 = (bf16[272,1024]{1,0:T(8,128)(2,1)}, bf16[272,1024]{1,0:T(8,128)(2,1)}, u32[]{:S(2)}, u32[]{:S(2)}) collective-permute-start(bf16[272,1024]{1,0:T(8,128)(2,1)} %get-tuple-element.103), channel_id=1, source_target_pairs={{0,8},{4,12},{8,16},{12,20},{16,24},{20,28},{24,0},{28,4},{1,9},{5... | collective-permute-start | bytes 1671176 | tf_op jit(solution)/shard_map/ppermute | solution.py:200
  374.3 36.6 %collective-permute-start.11 = (bf16[272,1024]{1,0:T(8,128)(2,1)}, bf16[272,1024]{1,0:T(8,128)(2,1)}, u32[]{:S(2)}, u32[]{:S(2)}) collective-permute-start(bf16[272,1024]{1,0:T(8,128)(2,1)} %get-tuple-element.102), channel_id=1, source_target_pairs={{0,12},{4,16},{8,20},{12,24},{16,28},{20,0},{24,4},{28,8},{1,13},{... | collective-permute-start | bytes 1671176 | tf_op jit(solution)/shard_map/ppermute | solution.py:200
  375.1 36.2 %collective-permute-start.12 = (bf16[272,1024]{1,0:T(8,128)(2,1)}, bf16[272,1024]{1,0:T(8,128)(2,1)S(1)}, u32[]{:S(2)}, u32[]{:S(2)}) collective-permute-start(bf16[272,1024]{1,0:T(8,128)(2,1)} %get-tuple-element.101), channel_id=1, source_target_pairs={{0,16},{4,20},{8,24},{12,28},{16,0},{20,4},{24,8},{28,12},{1,17},{... | collective-permute-start | bytes 1671176 | tf_op jit(solution)/shard_map/ppermute | solution.py:200
  376.0 54.3 %collective-permute-start.13 = (bf16[272,1024]{1,0:T(8,128)(2,1)}, bf16[272,1024]{1,0:T(8,128)(2,1)S(1)}, u32[]{:S(2)}, u32[]{:S(2)}) collective-permute-start(bf16[272,1024]{1,0:T(8,128)(2,1)} %get-tuple-element.100), channel_id=1, source_target_pairs={{0,20},{4,24},{8,28},{12,0},{16,4},{20,8},{24,12},{28,16},{1,21},{... | collective-permute-start | bytes 1671176 | tf_op jit(solution)/shard_map/ppermute | solution.py:200
  377.4 52.9 %collective-permute-start.14 = (bf16[272,1024]{1,0:T(8,128)(2,1)}, bf16[272,1024]{1,0:T(8,128)(2,1)S(1)}, u32[]{:S(2)}, u32[]{:S(2)}) collective-permute-start(bf16[272,1024]{1,0:T(8,128)(2,1)} %get-tuple-element.99), channel_id=1, source_target_pairs={{0,24},{4,28},{8,0},{12,4},{16,8},{20,12},{24,16},{28,20},{1,25},{... | collective-permute-start | bytes 1671176 | tf_op jit(solution)/shard_map/ppermute | solution.py:200
  389.5 40.8 %collective-permute-start.15 = (bf16[272,1024]{1,0:T(8,128)(2,1)S(1)}, bf16[272,1024]{1,0:T(8,128)(2,1)S(1)}, u32[]{:S(2)}, u32[]{:S(2)}) collective-permute-start(bf16[272,1024]{1,0:T(8,128)(2,1)S(1)} %get-tuple-element.98), channel_id=1, source_target_pairs={{0,28},{4,0},{8,4},{12,8},{16,12},{20,16},{24,20},{28,24},{1,29},{... | collective-permute-start | bytes 1671176 | tf_op jit(solution)/shard_map/ppermute | solution.py:200
  410.9 19.4 %collective-permute-start.9 = (bf16[272,1024]{1,0:T(8,128)(2,1)S(1)}, bf16[272,1024]{1,0:T(8,128)(2,1)S(1)}, u32[]{:S(2)}, u32[]{:S(2)}) collective-permute-start(bf16[272,1024]{1,0:T(8,128)(2,1)S(1)} %get-tuple-element.97), channel_id=1, source_target_pairs={{0,4},{4,8},{8,12},{12,16},{16,20},{20,24},{24,28},{28,0},{1,5},{5... | collective-permute-start | bytes 1671176 | tf_op jit(solution)/shard_map/ppermute | solution.py:200
  411.2 21.4 %copy-start.13 = (bf16[1152,1024]{1,0:T(8,128)(2,1)S(1)}, bf16[1152,1024]{1,0:T(8,128)(2,1)}, u32[]{:S(2)}) copy-start(bf16[1152,1024]{1,0:T(8,128)(2,1)} %get-tuple-element.96) | copy-start | bytes 7077892
  432.8 4.2 copy-start.17
  432.8 17.5 %collective-permute-start.16 = (bf16[1,288,1024]{2,1,0:T(8,128)(2,1)S(1)}, bf16[1,288,1024]{2,1,0:T(8,128)(2,1)S(1)}, u32[]{:S(2)}, u32[]{:S(2)}) collective-permute-start(bf16[1,288,1024]{2,1,0:T(8,128)(2,1)S(1)} %get-tuple-element.104), channel_id=1, source_target_pairs={{0,3},{1,0},{2,1},{3,2},{4,7},{5,4},{6,5},{7,6},{8,11},{9,8},{10,9... | collective-permute-start | bytes 1769480 | tf_op jit(solution)/shard_map/ppermute | solution.py:189
  434.4 51.4 %collective-permute-start.17 = (bf16[1,288,1024]{2,1,0:T(8,128)(2,1)S(1)}, bf16[1,288,1024]{2,1,0:T(8,128)(2,1)S(1)}, u32[]{:S(2)}, u32[]{:S(2)}) collective-permute-start(bf16[1,288,1024]{2,1,0:T(8,128)(2,1)S(1)} %get-tuple-element.106), channel_id=1, source_target_pairs={{0,2},{1,3},{2,0},{3,1},{4,6},{5,7},{6,4},{7,5},{8,10},{9,11},{10,... | collective-permute-start | bytes 1769480 | tf_op jit(solution)/shard_map/ppermute | solution.py:189
  434.4 51.4 %collective-permute-start.18 = (bf16[1,288,1024]{2,1,0:T(8,128)(2,1)S(1)}, bf16[1,288,1024]{2,1,0:T(8,128)(2,1)S(1)}, u32[]{:S(2)}, u32[]{:S(2)}) collective-permute-start(bf16[1,288,1024]{2,1,0:T(8,128)(2,1)S(1)} %get-tuple-element.105), channel_id=1, source_target_pairs={{0,1},{1,2},{2,3},{3,0},{4,5},{5,6},{6,7},{7,4},{8,9},{9,10},{10,1... | collective-permute-start | bytes 1769480 | tf_op jit(solution)/shard_map/ppermute | solution.py:189
  440.7 52.5 %copy-start.12 = (f32[288,1024]{1,0:T(8,128)S(1)}, f32[288,1024]{1,0:T(8,128)}, u32[]{:S(2)}) copy-start(f32[288,1024]{1,0:T(8,128)} %get-tuple-element.95) | copy-start | bytes 3538948
  487.7 13.8 %collective-permute-start.19 = (bf16[144,1792]{1,0:T(8,128)(2,1)S(1)}, bf16[144,1792]{1,0:T(8,128)(2,1)S(1)}, u32[]{:S(2)}, u32[]{:S(2)}) collective-permute-start(bf16[144,1792]{1,0:T(8,128)(2,1)S(1)} %get-tuple-element.120), channel_id=1, source_target_pairs={{0,3},{1,0},{2,1},{3,2},{4,7},{5,4},{6,5},{7,6},{8,11},{9,8},{10,9... | collective-permute-start | bytes 1548296 | tf_op jit(solution)/shard_map/ppermute | solution.py:189
  487.8 48.3 %collective-permute-start.20 = (bf16[144,1792]{1,0:T(8,128)(2,1)S(1)}, bf16[144,1792]{1,0:T(8,128)(2,1)S(1)}, u32[]{:S(2)}, u32[]{:S(2)}) collective-permute-start(bf16[144,1792]{1,0:T(8,128)(2,1)S(1)} %get-tuple-element.120), channel_id=1, source_target_pairs={{0,2},{1,3},{2,0},{3,1},{4,6},{5,7},{6,4},{7,5},{8,10},{9,11},{10,... | collective-permute-start | bytes 1548296 | tf_op jit(solution)/shard_map/ppermute | solution.py:189
  491.2 44.9 %collective-permute-start.21 = (bf16[144,1792]{1,0:T(8,128)(2,1)S(1)}, bf16[144,1792]{1,0:T(8,128)(2,1)S(1)}, u32[]{:S(2)}, u32[]{:S(2)}) collective-permute-start(bf16[144,1792]{1,0:T(8,128)(2,1)S(1)} %get-tuple-element.120), channel_id=1, source_target_pairs={{0,1},{1,2},{2,3},{3,0},{4,5},{5,6},{6,7},{7,4},{8,9},{9,10},{10,1... | collective-permute-start | bytes 1548296 | tf_op jit(solution)/shard_map/ppermute | solution.py:189
  541.0 5.8 %copy-start.1 = (bf16[512,1024]{1,0:T(8,128)(2,1)S(1)}, bf16[512,1024]{1,0:T(8,128)(2,1)}, u32[]{:S(2)}) copy-start(bf16[512,1024]{1,0:T(8,128)(2,1)} %param.28) | copy-start | bytes 3145732
  (6 other events, 9.3 us)
Sparse Core Ops, SparseCore 0:
  10.5 34.9 all-gather.6
  47.4 26.1 all-gather.8
  108.0 36.1 all-gather.12
  146.0 37.8 all-gather.10
  195.6 54.3 reduce-scatter.3
  253.5 99.9 all-reduce.10
  368.4 62.8 reduce-scatter.7
  435.0 41.4 reduce-scatter.5
